TPU v7x, 128 devices: a whole 4x4x4 slice. The times are simulated.
128 devices in a mesh: ctx: 8 (over x_lo, z), tp: 16 (over x_hi, y, core).
Axes of the slice: x: 4 (x_hi: 2, x_lo: 2; x = x_hi * 2 + x_lo), y: 4, z: 4, core: 2. Of those that a mesh axis runs over, the one named last changes fastest.
Arguments:
- in_gate: bfloat16 [4096, 4096], P('ctx', 'tp'), may hold values from -6 to 6
- value_stream: bfloat16 [4096, 4096], P('ctx', 'tp'), may hold values from -6 to 6
- out_gate: bfloat16 [4096, 4096], P('ctx', 'tp'), may hold values from -6 to 6
- residues: float32 [4096, 16], P('tp'), may hold values from -1.5 to 1.5
- decays: float32 [4096, 16], P('tp'), may hold values from 0.00024414062 to 0.05
- skip_gain: float32 [4096], P('tp'), may hold values from -3 to 3
- out_weight: bfloat16 [4096, 4096], P('tp'), may hold values from -0.09375 to 0.09375
Outputs:
- mixed: bfloat16 [4096, 4096], P(('ctx', 'tp'))
All inputs are finite; a program needn't handle non-finite values.
Results may differ from a plain program's by a relative error of at most 0.017.
Values may be sent and summed in bfloat16 or wider, within the bound.
A program may use at most 128 MiB of HBM per device.

v0:
```python
import math

import jax
import jax.numpy as jnp
from jax import lax
from jax.sharding import PartitionSpec as P


def contract(form, left, right):
    return jnp.einsum(form, left, right, precision=lax.Precision.HIGHEST)


def cosine_table(first, second, period):
    row_ids = lax.broadcasted_iota(jnp.int32, (first, second), 0)
    col_ids = lax.broadcasted_iota(jnp.int32, (first, second), 1)
    phases = row_ids * col_ids % period
    angles = phases.astype(jnp.float32) * (2.0 * math.pi / period)
    return (jnp.cos(angles), jnp.sin(angles))


def forward_spectrum(sig_real, sig_imag, lookup_tables):
    first_cos, first_sin, spin_cos, spin_sin, second_cos, second_sin = lookup_tables
    channels, length = sig_real.shape
    half_rows = first_cos.shape[1]
    grid_real = sig_real.reshape(channels, half_rows, length // half_rows)
    grid_imag = sig_imag.reshape(channels, half_rows, length // half_rows)
    section_real = contract("kn,cnm->ckm", first_cos, grid_real) + contract(
        "kn,cnm->ckm", first_sin, grid_imag
    )
    section_imag = contract("kn,cnm->ckm", first_cos, grid_imag) - contract(
        "kn,cnm->ckm", first_sin, grid_real
    )
    turned_real = section_real * spin_cos + section_imag * spin_sin
    turned_imag = section_imag * spin_cos - section_real * spin_sin
    out_real = contract("ckn,nm->ckm", turned_real, second_cos) + contract(
        "ckn,nm->ckm", turned_imag, second_sin
    )
    out_imag = contract("ckn,nm->ckm", turned_imag, second_cos) - contract(
        "ckn,nm->ckm", turned_real, second_sin
    )
    return (out_real, out_imag)


def reflected_rows(spectrum):
    rows_flipped = jnp.roll(jnp.flip(spectrum, 1), 1, axis=1)
    first_row = jnp.roll(jnp.flip(rows_flipped[:, :1, :], 2), 1, axis=2)
    other_rows = jnp.flip(rows_flipped[:, 1:, :], 2)
    return jnp.concatenate([first_row, other_rows], axis=1)


def inverse_pair(spec_real, spectrum_imaginary, lookup_tables, length):
    first_cos, first_sin, spin_cos, spin_sin, second_cos, second_sin = lookup_tables
    middle_real = contract("ckm,mn->ckn", spec_real, second_cos) - contract(
        "ckm,mn->ckn", spectrum_imaginary, second_sin
    )
    middle_imag = contract("ckm,mn->ckn", spectrum_imaginary, second_cos) + contract(
        "ckm,mn->ckn", spec_real, second_sin
    )
    back_real = middle_real * spin_cos - middle_imag * spin_sin
    back_imag = middle_imag * spin_cos + middle_real * spin_sin
    samples_real = contract("kn,ckm->cnm", first_cos, back_real) - contract(
        "kn,ckm->cnm", first_sin, back_imag
    )
    samples_imag = contract("kn,ckm->cnm", first_cos, back_imag) + contract(
        "kn,ckm->cnm", first_sin, back_real
    )
    pairs = spec_real.shape[0]
    scale = 1.0 / (2 * length)
    return (
        samples_real.reshape(pairs, length) * scale,
        samples_imag.reshape(pairs, length) * scale,
    )


def spectral_convolve(product):
    whole_rows = lax.all_to_all(product.T, "ctx", split_axis=0, concat_axis=1, tiled=True)
    return whole_rows


def transform_convolve(whole_rows, local_res, local_dec):
    narrow, length = whole_rows.shape
    amplitude = local_res * jnp.sqrt(2.0 * local_dec)
    positions = lax.broadcasted_iota(jnp.int32, (1, length), 1).astype(jnp.float32)

    def add_mode(mode_index, carried):
        mode_rate = lax.dynamic_slice_in_dim(local_dec, mode_index, 1, 1)
        mode_weight = lax.dynamic_slice_in_dim(amplitude, mode_index, 1, 1)
        return carried + mode_weight * jnp.exp(-mode_rate * positions)

    impulse = lax.fori_loop(
        0, local_dec.shape[1], add_mode, jnp.zeros((narrow, length), jnp.float32)
    )
    padded_len = 2 * length
    second_len = 256
    first_len = padded_len // second_len
    first_cos, first_sin = cosine_table(first_len, first_len // 2, first_len)
    spin_cos, spin_sin = cosine_table(first_len, second_len, padded_len)
    second_cos, second_sin = cosine_table(second_len, second_len, second_len)
    lookup_tables = (first_cos, first_sin, spin_cos, spin_sin, second_cos, second_sin)
    joint_real, joint_imag = forward_spectrum(
        whole_rows.astype(jnp.float32), impulse, lookup_tables
    )
    mirror_real = reflected_rows(joint_real)
    mirror_imag = reflected_rows(joint_imag)
    data_real = 0.5 * (joint_real + mirror_real)
    data_imag = 0.5 * (joint_imag - mirror_imag)
    kernel_real = 0.5 * (joint_imag + mirror_imag)
    kernel_imag = -0.5 * (joint_real - mirror_real)
    spec_real = data_real * kernel_real - data_imag * kernel_imag
    spectrum_imaginary = data_real * kernel_imag + data_imag * kernel_real
    freq_rows, freq_cols = (spec_real.shape[1], spec_real.shape[2])
    pair_real = spec_real.reshape(narrow // 2, 2, freq_rows, freq_cols)
    pair_imag = spectrum_imaginary.reshape(narrow // 2, 2, freq_rows, freq_cols)
    packed_real = pair_real[:, 0] - pair_imag[:, 1]
    packed_imag = pair_imag[:, 0] + pair_real[:, 1]
    even_rows, odd_rows = inverse_pair(packed_real, packed_imag, lookup_tables, length)
    return jnp.stack([even_rows, odd_rows], axis=1).reshape(narrow, length)


def body(in_gate, value_stream, out_gate, residues, decays, skip_gain, out_weight):
    product = (in_gate.astype(jnp.float32) * value_stream.astype(jnp.float32)).astype(jnp.bfloat16)
    whole_rows = spectral_convolve(product)
    narrow = whole_rows.shape[0]
    offset = lax.axis_index("ctx") * narrow
    local_res = lax.dynamic_slice_in_dim(residues, offset, narrow, 0)
    local_dec = lax.dynamic_slice_in_dim(decays, offset, narrow, 0)
    convolved = transform_convolve(whole_rows, local_res, local_dec)
    returned = lax.all_to_all(
        convolved.astype(jnp.bfloat16), "ctx", split_axis=1, concat_axis=0, tiled=True
    ).astype(convolved.dtype)
    gated = (
        out_gate.astype(jnp.float32) * (returned.T + skip_gain * product.astype(jnp.float32))
    ).astype(jnp.bfloat16)
    row_view = lax.all_to_all(gated, "tp", split_axis=0, concat_axis=1, tiled=True)
    block_width = out_weight.shape[0]
    out_rows = row_view.shape[0]
    out_width = out_weight.shape[1]
    piece = lax.all_gather(out_weight, "tp", axis=0, tiled=True)
    count = piece.shape[0] // block_width
    leading_blocks = row_view.reshape(out_rows, count, block_width)
    segment_blocks = piece.reshape(count, block_width, out_width)
    partial_value = jnp.einsum(
        "mex,exo->emo", leading_blocks, segment_blocks, preferred_element_type=jnp.float32
    )
    rounded = lax.optimization_barrier(partial_value.astype(jnp.bfloat16))
    mixed = jnp.sum(rounded.astype(jnp.float32), axis=0)
    return mixed.astype(jnp.bfloat16)


def solution(mesh):
    in_specs = (
        P("ctx", "tp"),
        P("ctx", "tp"),
        P("ctx", "tp"),
        P("tp", None),
        P("tp", None),
        P("tp"),
        P("tp", None),
    )
    out_specs = P(("ctx", "tp"), None)
    return jax.shard_map(body, mesh=mesh, in_specs=in_specs, out_specs=out_specs, check_vma=False)
```

profile of v0, /device:TPU:1, one launch (start us, length us, event | category | flops | bytes accessed | tf_op | source)
XLA Modules:
  0.0 231.3 jit_solution(2636801715747349479)
XLA Ops:
  7.3 1.1 copy.26
  8.4 1.1 copy.27
  10.2 6.8 %all-to-all-start = ((bf16[8,32,512]{2,1,0:T(8,128)(2,1)}), bf16[8,32,512]{2,1,0:T(8,128)(2,1)S(1)}, u32[]{:S(2)}, u32[]{:S(2)}) async-start(bf16[8,32,512]{2,1,0:T(8,128)(2,1)} %bitcast.1), calls=%async_computation | async-start | bytes 524288 | tf_op jit(solution)/shard_map/all_to_all | solution.py:76
  17.8 4.5 %while.14 = (s32[]{:T(128)}, f32[32,4096]{1,0:T(8,128)S(1)}, f32[32,16]{0,1:T(8,128)S(1)}, f32[32,16]{0,1:T(8,128)S(1)}, s32[]{:T(128)}, /*index=5*/s32[]{:T(128)}) while((s32[]{:T(128)}, f32[32,4096]{1,0:T(8,128)S(1)}, f32[32,16]{0,1:T(8,128)S(1)}, f32[32,16]{0,1:T(8,128)S(1)}, s32[]{:T(128)}, /*index=5*/s32[]{:T(128)}) %tuple.38), condition=%wide.region_1.0_spmd.clone, body=%wide.region_0.0_spmd.clone.sunk | while | flops 528419 | bytes 1082195 | solution.py:90
  26.5 2.0 fusion.17
  28.4 2.0 convolution_subtract_fusion
  30.4 1.2 slice.73
  31.8 2.0 fusion.16
  33.8 2.0 convolution_add_fusion
  35.7 1.1 slice.70
  37.6 2.0 rev.14
  41.5 2.6 %rev.13 = f32[32,31,256]{2,1,0:T(8,128)} reverse(f32[32,31,256]{2,1,0:T(8,128)} %slice.70), dimensions={1,2} | reverse | bytes 2031616 | tf_op jit(solution)/shard_map/jit(_flip)/rev | solution.py:47
  45.9 2.0 multiply_subtract_fusion
  47.9 1.6 fusion.26
  49.5 1.6 fusion.28
  51.0 1.6 convolution_add_fusion.2
  52.6 1.6 convolution_subtract_fusion.2
  57.9 5.1 %all-to-all-start.1 = ((bf16[32,8,512]{2,0,1:T(8,128)(2,1)}), bf16[32,8,512]{2,0,1:T(8,128)(2,1)S(1)}, u32[]{:S(2)}, u32[]{:S(2)}) async-start(bf16[32,8,512]{2,0,1:T(8,128)(2,1)} %copy.35), calls=%async_computation.1 | async-start | bytes 524288 | tf_op jit(solution)/shard_map/all_to_all | solution.py:128
  63.2 6.0 %all-to-all-done.1 = bf16[32,8,512]{2,0,1:T(8,128)(2,1)S(1)} async-done(((bf16[32,8,512]{2,0,1:T(8,128)(2,1)}), bf16[32,8,512]{2,0,1:T(8,128)(2,1)S(1)}, u32[]{:S(2)}, u32[]{:S(2)}) %all-to-all-start.1) | async-done | bytes 262176 | tf_op jit(solution)/shard_map/all_to_all | solution.py:128
  69.1 1.1 fusion.15
  70.4 20.7 %all_to_all.42 = bf16[16,32,256]{2,1,0:T(8,128)(2,1)S(1)} all-to-all(bf16[16,32,256]{2,1,0:T(8,128)(2,1)S(1)} %bitcast.133), channel_id=1, replica_groups=mesh['ctx'=8,'tp'=16] {'tp'}, dimensions={0} | all-to-all | bytes 524288 | tf_op jit(solution)/shard_map/all_to_all | solution.py:134
  91.1 111.2 %all-gather.2.cloned.1.call-done = bf16[4096,4096]{1,0:T(8,128)(2,1)} async-done(((bf16[256,4096]{1,0:T(8,128)(2,1)}), bf16[4096,4096]{1,0:T(8,128)(2,1)}) %all-gather.2.cloned.1.call-update) | async-done | bytes 33554448 | tf_op jit(solution)/shard_map/all_gather | solution.py:138
  202.3 18.5 %convolution_convert_fusion = bf16[16,32,4096]{2,1,0:T(8,128)(2,1)} fusion(bf16[16,256,4096]{2,1,0:T(8,128)(2,1)} %bitcast.119, bf16[16,32,256]{2,1,0:T(8,128)(2,1)S(1)} %all_to_all.42), kind=kOutput, calls=%fused_computation.5 | convolution fusion | flops 1075838976 | bytes 38010880 | tf_op jit(solution)/shard_map/mex,exo->emo/dot_general | solution.py:142
  220.8 3.7 %reduce_sum.12 = bf16[32,4096]{1,0:T(8,128)(2,1)} reduce(bf16[16,32,4096]{2,1,0:T(8,128)(2,1)} %convolution_convert_fusion, bf16[]{:T(256)} %constant.90.clone.1), dimensions={0}, to_apply=%region_2.3 | reduce | flops 1966080 | bytes 4456450 | tf_op jit(solution)/shard_map/reduce_sum | solution.py:146
  (83 shorter events, 18.8 us)
Async XLA Ops:
  6.5 56.5 %copy-start = (bf16[512,256]{1,0:T(8,128)(2,1)S(1)}, bf16[512,256]{1,0:T(8,128)(2,1)}, u32[]{:S(2)}) copy-start(bf16[512,256]{1,0:T(8,128)(2,1)} %param.11) | copy-start | bytes 786436
  6.5 195.8 %all-gather.2.cloned.1.call-start = ((), (), s32[]{:S(2)}) async-start(), calls=%async_computation.3 | async-start | bytes 35651584 | tf_op jit(solution)/shard_map/all_gather | solution.py:138
  10.2 13.5 %all-to-all-start = ((bf16[8,32,512]{2,1,0:T(8,128)(2,1)}), bf16[8,32,512]{2,1,0:T(8,128)(2,1)S(1)}, u32[]{:S(2)}, u32[]{:S(2)}) async-start(bf16[8,32,512]{2,1,0:T(8,128)(2,1)} %bitcast.1), calls=%async_computation | async-start | bytes 524288 | tf_op jit(solution)/shard_map/all_to_all | solution.py:76
  57.9 11.2 %all-to-all-start.1 = ((bf16[32,8,512]{2,0,1:T(8,128)(2,1)}), bf16[32,8,512]{2,0,1:T(8,128)(2,1)S(1)}, u32[]{:S(2)}, u32[]{:S(2)}) async-start(bf16[32,8,512]{2,0,1:T(8,128)(2,1)} %copy.35), calls=%async_computation.1 | async-start | bytes 524288 | tf_op jit(solution)/shard_map/all_to_all | solution.py:128
Sparse Core Ops, SparseCore 0:
  9.8 192.4 all-gather.1
where the time goes:
time: 232 us; the launch traced here: 231 us
  waiting for transfers between devices  118 us (51%)
  matrix products  38.1 us (16%)
  blocking collectives  20.7 us (9%)
  local copies, waits for them, and re-layouts  15.4 us (7%)
  between operations  13.7 us (6%)
  other arithmetic  13.1 us (6%)
  starting transfers between devices  11.9 us (5%)
    all_gather x1, waiting for transfers between devices, body(): piece = lax.all_gather(out_weight, 'tp', axis=0, tiled=True)  111 us
    all_to_all x1, blocking collectives, body(): lax.all_to_all(gated, 'tp', split_axis=0, concat_axis=1, tiled=True)  20.7 us
    dot_general x16, matrix products, contract(): return jnp.einsum(form, left, right, precision=lax.Precision.HIGHEST)  19.7 us
    dot_general x1, matrix products, body(): jnp.einsum('mex,exo->emo', leading_blocks, segment_blocks, preferred_elem...  18.5 us
    all_to_all x1, starting transfers between devices, spectral_convolve(): lax.all_to_all(product.T, 'ctx', split_axis=0, concat_axis=1, tiled=True)  6.79 us
    unnamed x10, local copies, waits for them, and re-layouts  6.24 us
    all_to_all x1, waiting for transfers between devices, body(): lax.all_to_all(convolved.astype(jnp.bfloat16), 'ctx', split_axis=1, conca...  5.95 us
    all_to_all x1, starting transfers between devices, body(): lax.all_to_all(convolved.astype(jnp.bfloat16), 'ctx', split_axis=1, conca...  5.13 us
  transfers between devices with their start and end apart: 3, of which 2 were waited for; matrix products, arithmetic and copies ran while one was open for 19% of the time, Pallas kernels for 0%

commit v1 on v0

v1 whole, which is shorter than its diff:
```python
import functools

import jax
import jax.numpy as jnp
from jax import lax
from jax.experimental import pallas as pl
from jax.experimental.pallas import tpu as pltpu
from jax.sharding import PartitionSpec as P

MESH = pl.DeviceIdType.MESH
F32 = jnp.float32
BF16 = jnp.bfloat16

LANES = 128
SUB = 8
YS = 4
PIECES = 8


def kernel(
    in_hbm, val_hbm, gate_hbm, res_ref, dec_ref, skip_ref, w_hbm, out_ref,
    ig, vs, og, w2, px, py, prefix, states, g_out, g2, part, rel, drt, com, x_out, x_in, acc,
    load_sem, st_send, st_recv, pair_send, pair_recv, rel_sem, drt_sem, com_sem, x_sem,
):
    tokens, chans = px.shape[1], px.shape[0] * LANES
    steps = tokens // SUB
    modes = res_ref.shape[0]
    n_ctx = states.shape[0]
    groups = chans // LANES
    rows = out_ref.shape[0]
    wide = part.shape[2]

    ctx = lax.axis_index("ctx")
    tp = lax.axis_index("tp")
    core = lax.rem(tp, 2)
    y = lax.rem(lax.div(tp, 2), YS)
    xh = lax.div(tp, 2 * YS)

    def device(ctx_i, xh_i, y_i, core_i):
        return (ctx_i, (xh_i * YS + y_i) * 2 + core_i)

    partner = device(ctx, xh, y, 1 - core)
    up = device(ctx, xh, lax.rem(y + 1, YS), core)
    down = device(ctx, xh, lax.rem(y + YS - 1, YS), core)
    across = device(ctx, 1 - xh, y, core)
    others = [(lax.rem(ctx + k, n_ctx), tp) for k in range(1, n_ctx)]

    barrier = pltpu.get_barrier_semaphore()
    peers = [partner, up, down, across] + others
    for peer in peers:
        pl.semaphore_signal(barrier, inc=1, device_id=peer, device_id_type=MESH)

    loads = [
        pltpu.make_async_copy(in_hbm, ig, load_sem.at[0]),
        pltpu.make_async_copy(val_hbm, vs, load_sem.at[1]),
        pltpu.make_async_copy(gate_hbm, og, load_sem.at[2]),
        pltpu.make_async_copy(w_hbm, w2.at[pl.ds(0, chans)], load_sem.at[3]),
    ]
    for load in loads:
        load.start()
    loads[0].wait()
    loads[1].wait()

    for g in range(groups):
        lanes = pl.ds(g * LANES, LANES)
        product = (ig[:, lanes].astype(F32) * vs[:, lanes].astype(F32)).astype(BF16)
        px[g] = product.astype(F32)

    def spread(row):
        return jnp.broadcast_to(row, (SUB, LANES))

    position = lax.broadcasted_iota(jnp.int32, (SUB, LANES), 0)
    place = position.astype(F32)

    def group_decay(g):
        decay = dec_ref[:, pl.ds(g * LANES, LANES)]
        return decay, jnp.exp(-decay)

    for g in range(groups):
        lanes = pl.ds(g * LANES, LANES)
        decay, step_factor = group_decay(g)
        factors = [spread(step_factor[m : m + 1]) for m in range(modes)]

        def advance(i, held, factors=factors, g=g):
            x = px[g, pl.ds(i, SUB, stride=steps), :]
            return tuple(f * s + x for f, s in zip(factors, held))

        zero = jnp.zeros((SUB, LANES), F32)
        ends = lax.fori_loop(0, steps, advance, (zero,) * modes, unroll=8)
        for m in range(modes):
            rate = spread(decay[m : m + 1])
            tail = jnp.exp(-rate * ((SUB - 1 - place) * steps))
            states[ctx, m : m + 1, lanes] = jnp.sum(tail * ends[m], axis=0, keepdims=True)
            scan = jnp.where(position >= 1, pltpu.roll(ends[m], 1, 0), 0.0)
            for hop in (1, 2, 4):
                weight = jnp.where(position >= hop, jnp.exp(-rate * (hop * steps)), 0.0)
                scan = scan + weight * pltpu.roll(scan, hop, 0)
            prefix[g, m] = scan

    pl.semaphore_wait(barrier, len(peers))
    state_copies = []
    for k, peer in enumerate(others):
        copy = pltpu.make_async_remote_copy(
            src_ref=states.at[ctx], dst_ref=states.at[ctx],
            send_sem=st_send.at[k], recv_sem=st_recv.at[k],
            device_id=peer, device_id_type=MESH,
        )
        copy.start()
        state_copies.append(copy)
    w_copy = pltpu.make_async_remote_copy(
        src_ref=w_hbm, dst_ref=w2.at[pl.ds(chans, chans)],
        send_sem=pair_send.at[0], recv_sem=pair_recv.at[0],
        device_id=partner, device_id_type=MESH,
    )
    w_copy.start()

    for g in range(groups):
        lanes = pl.ds(g * LANES, LANES)
        decay, step_factor = group_decay(g)
        amplitude = res_ref[:, lanes] * jnp.sqrt(2.0 * decay)
        factors = [spread(step_factor[m : m + 1]) for m in range(modes)]
        gains = [spread(amplitude[m : m + 1]) for m in range(modes)]

        def convolve(i, held, factors=factors, gains=gains, g=g):
            rows_i = pl.ds(i, SUB, stride=steps)
            x = px[g, rows_i, :]
            held = tuple(f * s + x for f, s in zip(factors, held))
            terms = [r * s for r, s in zip(gains, held)]
            while len(terms) > 1:
                terms = [terms[j] + terms[j + 1] for j in range(0, len(terms), 2)]
            py[g, rows_i, :] = terms[0]
            return held

        lax.fori_loop(0, steps, convolve, tuple(prefix[g, m] for m in range(modes)), unroll=4)

    for copy in state_copies:
        copy.wait_recv()

    for g in range(groups):
        lanes = pl.ds(g * LANES, LANES)
        decay, step_factor = group_decay(g)
        amplitude = res_ref[:, lanes] * jnp.sqrt(2.0 * decay)
        block_factor = jnp.exp(-decay * float(tokens))
        carried = jnp.zeros((modes, LANES), F32)
        for i in range(n_ctx - 1):
            carried = jnp.where(i < ctx, block_factor * carried + states[i, :, lanes], carried)
        carried = carried * amplitude
        factors = [spread(step_factor[m : m + 1]) for m in range(modes)]
        fades = tuple(
            spread(carried[m : m + 1]) * jnp.exp(-spread(decay[m : m + 1]) * (place * steps + 1.0))
            for m in range(modes)
        )

        def extend(i, fades, factors=factors, g=g):
            rows_i = pl.ds(i, SUB, stride=steps)
            terms = list(fades)
            while len(terms) > 1:
                terms = [terms[j] + terms[j + 1] for j in range(0, len(terms), 2)]
            py[g, rows_i, :] = py[g, rows_i, :] + terms[0]
            return tuple(f * v for f, v in zip(factors, fades))

        lax.fori_loop(0, steps, extend, fades, unroll=4)

    loads[2].wait()

    def gated_rows(block, g):
        at = pl.ds(pl.multiple_of(block * rows, rows), rows)
        lanes = pl.ds(g * LANES, LANES)
        gate = og[at, lanes].astype(F32)
        return (gate * (py[g, at, :] + skip_ref[:, lanes] * px[g, at, :])).astype(BF16)

    def target_block(r, q, core_i):
        xh_t = lax.rem(xh + q, 2)
        return (xh_t * YS + lax.rem(y + r, YS)) * 2 + core_i

    for r in range(YS):
        for q in range(2):
            for g in range(groups):
                g_out[pl.ds((2 * r + q) * rows, rows), pl.ds(g * LANES, LANES)] = gated_rows(
                    target_block(r, q, 1 - core), g
                )
    g_copy = pltpu.make_async_remote_copy(
        src_ref=g_out, dst_ref=g2.at[:, pl.ds(chans, chans)],
        send_sem=pair_send.at[1], recv_sem=pair_recv.at[1],
        device_id=partner, device_id_type=MESH,
    )
    g_copy.start()
    for r in range(YS):
        for q in range(2):
            for g in range(groups):
                g2[pl.ds((2 * r + q) * rows, rows), pl.ds(g * LANES, LANES)] = gated_rows(
                    target_block(r, q, core), g
                )
    loads[3].wait()
    w_copy.wait_recv()
    g_copy.wait_recv()

    pair = 2 * rows

    def block_rows(r):
        return pl.ds(r * pair, pair)

    def sends(p, odd):
        near, far, off, back = (3, 2, down, up) if odd else (1, 2, up, down)
        rel_copy = functools.partial(
            pltpu.make_async_remote_copy,
            src_ref=part.at[p, block_rows(far)], dst_ref=rel.at[p],
            send_sem=rel_sem.at[0, p], recv_sem=rel_sem.at[1, p],
            device_id=off, device_id_type=MESH,
        )
        drt_copy = functools.partial(
            pltpu.make_async_remote_copy,
            src_ref=part.at[p, block_rows(4 - near)], dst_ref=drt.at[p],
            send_sem=drt_sem.at[0, p], recv_sem=drt_sem.at[1, p],
            device_id=back, device_id_type=MESH,
        )
        com_copy = functools.partial(
            pltpu.make_async_remote_copy,
            src_ref=part.at[p, block_rows(near)], dst_ref=com.at[p],
            send_sem=com_sem.at[0, p], recv_sem=com_sem.at[1, p],
            device_id=off, device_id_type=MESH,
        )
        x_copy = functools.partial(
            pltpu.make_async_remote_copy,
            src_ref=x_out.at[p], dst_ref=x_in.at[p],
            send_sem=x_sem.at[0, p], recv_sem=x_sem.at[1, p],
            device_id=across, device_id_type=MESH,
        )
        return near, rel_copy, drt_copy, com_copy, x_copy

    def multiply(j, carry):
        for odd in (0, 1):
            p = 2 * j + odd
            cols = pl.ds(pl.multiple_of(p * wide, wide), wide)
            part[p] = jnp.dot(g2[...], w2[:, cols], preferred_element_type=F32).astype(BF16)
            _, rel_copy, drt_copy, _, _ = sends(p, odd)
            rel_copy().start()
            drt_copy().start()
        return carry

    lax.fori_loop(0, PIECES // 2, multiply, 0)

    def relay(j, carry):
        for odd in (0, 1):
            p = 2 * j + odd
            near, rel_copy, _, com_copy, _ = sends(p, odd)
            rel_copy().wait_recv()
            at = block_rows(near)
            part[p, at] = (part[p, at].astype(F32) + rel[p].astype(F32)).astype(BF16)
            com_copy().start()
        return carry

    lax.fori_loop(0, PIECES // 2, relay, 0)

    def gather(j, carry):
        for odd in (0, 1):
            p = 2 * j + odd
            _, _, drt_copy, com_copy, x_copy = sends(p, odd)
            drt_copy().wait_recv()
            com_copy().wait_recv()
            total = part[p, block_rows(0)].astype(F32) + drt[p].astype(F32) + com[p].astype(F32)
            x_out[p] = total[rows:].astype(BF16)
            x_copy().start()
            acc[p] = total[:rows]
        return carry

    lax.fori_loop(0, PIECES // 2, gather, 0)

    def finish(j, carry):
        for odd in (0, 1):
            p = 2 * j + odd
            _, rel_copy, drt_copy, com_copy, x_copy = sends(p, odd)
            x_copy().wait_recv()
            cols = pl.ds(pl.multiple_of(p * wide, wide), wide)
            out_ref[:, cols] = (acc[p] + x_in[p].astype(F32)).astype(BF16)
            rel_copy().wait_send()
            drt_copy().wait_send()
            com_copy().wait_send()
            x_copy().wait_send()
        return carry

    lax.fori_loop(0, PIECES // 2, finish, 0)
    for copy in state_copies:
        copy.wait_send()
    w_copy.wait_send()
    g_copy.wait_send()


def body(n_ctx, n_tp, in_gate, value_stream, out_gate, residues, decays, skip_gain, out_weight):
    tokens, chans = in_gate.shape
    modes = residues.shape[1]
    width = out_weight.shape[1]
    rows = tokens // n_tp
    wide = width // PIECES
    groups = chans // LANES
    any_space = pl.BlockSpec(memory_space=pl.ANY)
    vmem = pl.BlockSpec(memory_space=pltpu.VMEM)
    dma = pltpu.SemaphoreType.DMA
    return pl.pallas_call(
        kernel,
        out_shape=jax.ShapeDtypeStruct((rows, width), BF16),
        in_specs=[any_space] * 3 + [vmem] * 3 + [any_space],
        out_specs=vmem,
        scratch_shapes=[
            pltpu.VMEM((tokens, chans), BF16),
            pltpu.VMEM((tokens, chans), BF16),
            pltpu.VMEM((tokens, chans), BF16),
            pltpu.VMEM((2 * chans, width), BF16),
            pltpu.VMEM((groups, tokens, LANES), F32),
            pltpu.VMEM((groups, tokens, LANES), F32),
            pltpu.VMEM((groups, modes, SUB, LANES), F32),
            pltpu.VMEM((n_ctx, modes, chans), F32),
            pltpu.VMEM((tokens // 2, chans), BF16),
            pltpu.VMEM((tokens // 2, 2 * chans), BF16),
            pltpu.VMEM((PIECES, tokens // 2, wide), BF16),
            pltpu.VMEM((PIECES, 2 * rows, wide), BF16),
            pltpu.VMEM((PIECES, 2 * rows, wide), BF16),
            pltpu.VMEM((PIECES, 2 * rows, wide), BF16),
            pltpu.VMEM((PIECES, rows, wide), BF16),
            pltpu.VMEM((PIECES, rows, wide), BF16),
            pltpu.VMEM((PIECES, rows, wide), F32),
            dma((4,)),
            dma((n_ctx - 1,)),
            dma((n_ctx - 1,)),
            dma((2,)),
            dma((2,)),
            dma((2, PIECES)),
            dma((2, PIECES)),
            dma((2, PIECES)),
            dma((2, PIECES)),
        ],
        compiler_params=pltpu.CompilerParams(
            collective_id=0, has_side_effects=True, vmem_limit_bytes=48 * 1024 * 1024
        ),
        cost_estimate=pl.CostEstimate(
            flops=2 * tokens * chans * width, bytes_accessed=4 * 1024 * 1024, transcendentals=0
        ),
    )(
        in_gate, value_stream, out_gate, residues.T, decays.T,
        skip_gain.reshape(1, chans), out_weight,
    )


def solution(mesh):
    n_ctx, n_tp = mesh.shape["ctx"], mesh.shape["tp"]
    in_specs = (
        P("ctx", "tp"),
        P("ctx", "tp"),
        P("ctx", "tp"),
        P("tp", None),
        P("tp", None),
        P("tp"),
        P("tp", None),
    )
    out_specs = P(("ctx", "tp"), None)
    return jax.shard_map(
        functools.partial(body, n_ctx, n_tp),
        mesh=mesh, in_specs=in_specs, out_specs=out_specs, check_vma=False,
    )
```

time: 232 us -> 45.9 us (0.20)
  waiting for transfers between devices: 118 us -> 0 us
  Pallas kernels: 0 us -> 38.3 us
  matrix products: 38.1 us -> 0 us
  blocking collectives: 20.7 us -> 0 us
  between operations: 13.7 us -> 0.02 us
  other arithmetic: 13.1 us -> 0 us
  starting transfers between devices: 11.9 us -> 0 us
  local copies, waits for them, and re-layouts: 15.4 us -> 7.26 us
    all_gather x1 -> x0, waiting for transfers between devices: 111 us -> none  [body(): piece = lax.all_gather(out_weight, 'tp', axis=0, tiled=True)]
    pallas_call x0 -> x1, Pallas kernels: none -> 38.3 us  [body(): pl.pallas_call(kernel, out_shape=jax.ShapeDtypeStruct((rows, width), BF16...]
    dot_general x17 -> x0, matrix products: 38.1 us -> none  [the longest x16 19.7 us: contract(): return jnp.einsum(form, left, right, precision=lax.Precision.HIGHEST)]
    all_to_all x1 -> x0, blocking collectives: 20.7 us -> none  [body(): lax.all_to_all(gated, 'tp', split_axis=0, concat_axis=1, tiled=True)]
    all_to_all x2 -> x0, starting transfers between devices: 11.9 us -> none  [the longest x1 6.79 us: spectral_convolve(): lax.all_to_all(product.T, 'ctx', split_axis=0, concat_axis=1, tiled=True)]
    all_to_all x2 -> x0, waiting for transfers between devices: 5.95 us -> none  [the longest x1 5.95 us: body(): lax.all_to_all(convolved.astype(jnp.bfloat16), 'ctx', split_axis=1, conca...]
    rev x2 -> x0, local copies, waits for them, and re-layouts: 4.52 us -> none  [reflected_rows(): other_rows = jnp.flip(rows_flipped[:, 1:, :], 2)]
    reduce_sum x1 -> x0, other arithmetic: 3.72 us -> none  [body(): mixed = jnp.sum(rounded.astype(jnp.float32), axis=0)]
  transfers between devices with their start and end apart: 3 -> 0, of which waited for: 2 -> 0; matrix products, arithmetic and copies ran while one was open for 19% -> 0% of each run, Pallas kernels for 0% -> 0%
where the time goes in v1:
time: 45.9 us; the launch traced here: 45.6 us
  Pallas kernels  38.3 us (83%)
  local copies, waits for them, and re-layouts  7.26 us (16%)
    pallas_call x1, Pallas kernels, body(): pl.pallas_call(kernel, out_shape=jax.ShapeDtypeStruct((rows, width), BF16...  38.3 us
    unnamed x15, local copies, waits for them, and re-layouts  7.26 us

profile of v1, /device:TPU:1, one launch (start us, length us, event | category | flops | bytes accessed | tf_op | source)
XLA Modules:
  0.0 45.6 jit_solution(2222959700659167506)
XLA Ops:
  0.0 0.0 copy-start
  0.0 1.6 %copy-done = bf16[256,4096]{1,0:T(8,128)(2,1)S(1)} copy-done((bf16[256,4096]{1,0:T(8,128)(2,1)S(1)}, bf16[256,4096]{1,0:T(8,128)(2,1)}, u32[]{:S(2)}) %copy-start) | copy-done | bytes 2097176
  1.6 0.0 copy-start.1
  1.6 0.9 %copy-done.1 = bf16[512,256]{1,0:T(8,128)(2,1)S(1)} copy-done((bf16[512,256]{1,0:T(8,128)(2,1)S(1)}, bf16[512,256]{1,0:T(8,128)(2,1)}, u32[]{:S(2)}) %copy-start.1) | copy-done | bytes 262168
  2.5 0.0 copy-start.2
  2.5 0.9 %copy-done.2 = bf16[512,256]{1,0:T(8,128)(2,1)S(1)} copy-done((bf16[512,256]{1,0:T(8,128)(2,1)S(1)}, bf16[512,256]{1,0:T(8,128)(2,1)}, u32[]{:S(2)}) %copy-start.2) | copy-done | bytes 262168
  3.5 0.0 copy-start.3
  3.5 0.9 %copy-done.3 = bf16[512,256]{1,0:T(8,128)(2,1)S(1)} copy-done((bf16[512,256]{1,0:T(8,128)(2,1)S(1)}, bf16[512,256]{1,0:T(8,128)(2,1)}, u32[]{:S(2)}) %copy-start.3) | copy-done | bytes 262168
  4.4 0.0 copy-start.4
  4.4 0.7 %copy-done.4 = f32[256,16]{0,1:T(8,128)S(1)} copy-done((f32[256,16]{0,1:T(8,128)S(1)}, f32[256,16]{0,1:T(8,128)}, u32[]{:S(2)}) %copy-start.4) | copy-done | bytes 16408
  5.2 0.0 copy-start.5
  5.2 0.7 %copy-done.5 = f32[256,16]{0,1:T(8,128)S(1)} copy-done((f32[256,16]{0,1:T(8,128)S(1)}, f32[256,16]{0,1:T(8,128)}, u32[]{:S(2)}) %copy-start.5) | copy-done | bytes 16408
  5.9 0.0 copy-start.6
  5.9 0.7 %copy-done.6 = f32[256]{0:T(256)S(1)} copy-done((f32[256]{0:T(256)S(1)}, f32[256]{0:T(256)}, u32[]{:S(2)}) %copy-start.6) | copy-done | bytes 1048
  6.6 38.3 %shard_map.73 = bf16[32,4096]{1,0:T(8,128)(2,1)S(1)} custom-call(bf16[512,256]{1,0:T(8,128)(2,1)S(1)} %copy-done.1, bf16[512,256]{1,0:T(8,128)(2,1)S(1)} %copy-done.2, bf16[512,256]{1,0:T(8,128)(2,1)S(1)} %copy-done.3, f32[16,256]{1,0:T(8,128)S(1)} %bitcast.3, f32[16,256]{1,0:T(8,128)S(1)} %bitcast.4, f32[1,256]{1,0:T(1,128)S(1)} %bitcast.5, ...), custom_call_target="tpu_custom_call" | custom-call | flops 1073741824 | bytes 4194304 | tf_op jit(solution)/shard_map/pallas_call | solution.py:299
  44.9 0.7 %copy.9 = bf16[32,4096]{1,0:T(8,128)(2,1)} copy(bf16[32,4096]{1,0:T(8,128)(2,1)S(1)} %shard_map.73) | data formatting | bytes 524288
Async XLA Ops:
  0.0 1.6 %copy-start = (bf16[256,4096]{1,0:T(8,128)(2,1)S(1)}, bf16[256,4096]{1,0:T(8,128)(2,1)}, u32[]{:S(2)}) copy-start(bf16[256,4096]{1,0:T(8,128)(2,1)} %w_hbm.1) | copy-start | bytes 6291460
  1.6 0.9 %copy-start.1 = (bf16[512,256]{1,0:T(8,128)(2,1)S(1)}, bf16[512,256]{1,0:T(8,128)(2,1)}, u32[]{:S(2)}) copy-start(bf16[512,256]{1,0:T(8,128)(2,1)} %in_hbm.1) | copy-start | bytes 786436
  2.5 0.9 %copy-start.2 = (bf16[512,256]{1,0:T(8,128)(2,1)S(1)}, bf16[512,256]{1,0:T(8,128)(2,1)}, u32[]{:S(2)}) copy-start(bf16[512,256]{1,0:T(8,128)(2,1)} %val_hbm.1) | copy-start | bytes 786436
  3.5 0.9 %copy-start.3 = (bf16[512,256]{1,0:T(8,128)(2,1)S(1)}, bf16[512,256]{1,0:T(8,128)(2,1)}, u32[]{:S(2)}) copy-start(bf16[512,256]{1,0:T(8,128)(2,1)} %gate_hbm.1) | copy-start | bytes 786436
  4.4 0.7 %copy-start.4 = (f32[256,16]{0,1:T(8,128)S(1)}, f32[256,16]{0,1:T(8,128)}, u32[]{:S(2)}) copy-start(f32[256,16]{0,1:T(8,128)} %param.10) | copy-start | bytes 49156
  5.2 0.7 %copy-start.5 = (f32[256,16]{0,1:T(8,128)S(1)}, f32[256,16]{0,1:T(8,128)}, u32[]{:S(2)}) copy-start(f32[256,16]{0,1:T(8,128)} %param.11) | copy-start | bytes 49156
  5.9 0.7 %copy-start.6 = (f32[256]{0:T(256)S(1)}, f32[256]{0:T(256)}, u32[]{:S(2)}) copy-start(f32[256]{0:T(256)} %param.12) | copy-start | bytes 3076

commit v2 on v1

--- a/solution.py
+++ b/solution.py
@@ -14,13 +14,14 @@
 LANES = 128
 SUB = 8
 YS = 4
-PIECES = 8
+X_PIECES, Y_PIECES = 7, 9
 
 
 def kernel(
-    in_hbm, val_hbm, gate_hbm, res_ref, dec_ref, skip_ref, w_hbm, out_ref,
-    ig, vs, og, w2, px, py, prefix, states, g_out, g2, part, rel, drt, com, x_out, x_in, acc,
-    load_sem, st_send, st_recv, pair_send, pair_recv, rel_sem, drt_sem, com_sem, x_sem,
+    in_hbm, val_hbm, gate_hbm, res_hbm, dec_hbm, skip_hbm, w_hbm, out_ref,
+    res_ref, dec_ref, skip_ref, ig, vs, og, w2, px, py, prefix, states, g_out, g2, part,
+    x_in, x_rel, x_drt, x_com, y_rel, y_drt, y_com, y_out, y_in, acc,
+    load_sem, st_send, st_recv, pair_send, pair_recv, x_sem, y_sem,
 ):
     tokens, chans = px.shape[1], px.shape[0] * LANES
     steps = tokens // SUB
@@ -28,7 +29,7 @@
     n_ctx = states.shape[0]
     groups = chans // LANES
     rows = out_ref.shape[0]
-    wide = part.shape[2]
+    wide = part.shape[3]
 
     ctx = lax.axis_index("ctx")
     tp = lax.axis_index("tp")
@@ -50,13 +51,18 @@
     for peer in peers:
         pl.semaphore_signal(barrier, inc=1, device_id=peer, device_id_type=MESH)
 
+    small = [
+        pltpu.make_async_copy(dec_hbm, dec_ref, load_sem.at[4]),
+        pltpu.make_async_copy(res_hbm, res_ref, load_sem.at[5]),
+        pltpu.make_async_copy(skip_hbm, skip_ref, load_sem.at[6]),
+    ]
     loads = [
         pltpu.make_async_copy(in_hbm, ig, load_sem.at[0]),
         pltpu.make_async_copy(val_hbm, vs, load_sem.at[1]),
         pltpu.make_async_copy(gate_hbm, og, load_sem.at[2]),
         pltpu.make_async_copy(w_hbm, w2.at[pl.ds(0, chans)], load_sem.at[3]),
     ]
-    for load in loads:
+    for load in loads[:2] + small + loads[2:]:
         load.start()
     loads[0].wait()
     loads[1].wait()
@@ -75,6 +81,9 @@
     def group_decay(g):
         decay = dec_ref[:, pl.ds(g * LANES, LANES)]
         return decay, jnp.exp(-decay)
+
+    for load in small:
+        load.wait()
 
     for g in range(groups):
         lanes = pl.ds(g * LANES, LANES)
@@ -176,7 +185,7 @@
     for r in range(YS):
         for q in range(2):
             for g in range(groups):
-                g_out[pl.ds((2 * r + q) * rows, rows), pl.ds(g * LANES, LANES)] = gated_rows(
+                g_out[pl.ds((q * YS + r) * rows, rows), pl.ds(g * LANES, LANES)] = gated_rows(
                     target_block(r, q, 1 - core), g
                 )
     g_copy = pltpu.make_async_remote_copy(
@@ -188,98 +197,132 @@
     for r in range(YS):
         for q in range(2):
             for g in range(groups):
-                g2[pl.ds((2 * r + q) * rows, rows), pl.ds(g * LANES, LANES)] = gated_rows(
+                g2[pl.ds((q * YS + r) * rows, rows), pl.ds(g * LANES, LANES)] = gated_rows(
                     target_block(r, q, core), g
                 )
     loads[3].wait()
     w_copy.wait_recv()
     g_copy.wait_recv()
 
-    pair = 2 * rows
-
-    def block_rows(r):
-        return pl.ds(r * pair, pair)
-
-    def sends(p, odd):
-        near, far, off, back = (3, 2, down, up) if odd else (1, 2, up, down)
-        rel_copy = functools.partial(
-            pltpu.make_async_remote_copy,
-            src_ref=part.at[p, block_rows(far)], dst_ref=rel.at[p],
-            send_sem=rel_sem.at[0, p], recv_sem=rel_sem.at[1, p],
-            device_id=off, device_id_type=MESH,
+    half = YS * rows
+    n_x, n_y = x_in.shape[0], y_in.shape[0]
+
+    def send(src, dst, sems, k, to):
+        return pltpu.make_async_remote_copy(
+            src_ref=src, dst_ref=dst, send_sem=sems.at[0, k], recv_sem=sems.at[1, k],
+            device_id=to, device_id_type=MESH,
         )
-        drt_copy = functools.partial(
-            pltpu.make_async_remote_copy,
-            src_ref=part.at[p, block_rows(4 - near)], dst_ref=drt.at[p],
-            send_sem=drt_sem.at[0, p], recv_sem=drt_sem.at[1, p],
-            device_id=back, device_id_type=MESH,
+
+    def neighbour(turn):
+        return device(ctx, xh, lax.rem(y + 1 + 2 * turn, YS), core)
+
+    def block(r):
+        return pl.ds(r * rows, rows)
+
+    def y_first(k):
+        turn = lax.rem(k, 2)
+        p = n_x + k
+        src = part.at[p]
+        return (
+            p, 1 + 2 * turn,
+            functools.partial(send, src.at[:, block(2)], y_rel.at[k], y_sem.at[0], k, neighbour(turn)),
+            functools.partial(send, src.at[:, block(3 - 2 * turn)], y_drt.at[k], y_sem.at[1], k, neighbour(1 - turn)),
+            functools.partial(send, src.at[:, block(1 + 2 * turn)], y_com.at[k], y_sem.at[2], k, neighbour(turn)),
+            functools.partial(send, y_out.at[k], y_in.at[k], y_sem.at[3], k, across),
         )
-        com_copy = functools.partial(
-            pltpu.make_async_remote_copy,
-            src_ref=part.at[p, block_rows(near)], dst_ref=com.at[p],
-            send_sem=com_sem.at[0, p], recv_sem=com_sem.at[1, p],
-            device_id=off, device_id_type=MESH,
+
+    def x_first(k):
+        turn = lax.rem(k + 1, 2)
+        src = part.at[k, 0]
+        return (
+            1 + 2 * turn,
+            functools.partial(send, src.at[block(2)], x_rel.at[k], x_sem.at[0], k, neighbour(turn)),
+            functools.partial(send, src.at[block(3 - 2 * turn)], x_drt.at[k], x_sem.at[1], k, neighbour(1 - turn)),
+            functools.partial(send, src.at[block(1 + 2 * turn)], x_com.at[k], x_sem.at[2], k, neighbour(turn)),
+            functools.partial(send, part.at[k, 1], x_in.at[k], x_sem.at[3], k, across),
         )
-        x_copy = functools.partial(
-            pltpu.make_async_remote_copy,
-            src_ref=x_out.at[p], dst_ref=x_in.at[p],
-            send_sem=x_sem.at[0, p], recv_sem=x_sem.at[1, p],
-            device_id=across, device_id_type=MESH,
-        )
-        return near, rel_copy, drt_copy, com_copy, x_copy
-
-    def multiply(j, carry):
-        for odd in (0, 1):
-            p = 2 * j + odd
-            cols = pl.ds(pl.multiple_of(p * wide, wide), wide)
-            part[p] = jnp.dot(g2[...], w2[:, cols], preferred_element_type=F32).astype(BF16)
-            _, rel_copy, drt_copy, _, _ = sends(p, odd)
-            rel_copy().start()
-            drt_copy().start()
-        return carry
-
-    lax.fori_loop(0, PIECES // 2, multiply, 0)
-
-    def relay(j, carry):
-        for odd in (0, 1):
-            p = 2 * j + odd
-            near, rel_copy, _, com_copy, _ = sends(p, odd)
-            rel_copy().wait_recv()
-            at = block_rows(near)
-            part[p, at] = (part[p, at].astype(F32) + rel[p].astype(F32)).astype(BF16)
-            com_copy().start()
-        return carry
-
-    lax.fori_loop(0, PIECES // 2, relay, 0)
-
-    def gather(j, carry):
-        for odd in (0, 1):
-            p = 2 * j + odd
-            _, _, drt_copy, com_copy, x_copy = sends(p, odd)
-            drt_copy().wait_recv()
-            com_copy().wait_recv()
-            total = part[p, block_rows(0)].astype(F32) + drt[p].astype(F32) + com[p].astype(F32)
-            x_out[p] = total[rows:].astype(BF16)
-            x_copy().start()
-            acc[p] = total[:rows]
-        return carry
-
-    lax.fori_loop(0, PIECES // 2, gather, 0)
-
-    def finish(j, carry):
-        for odd in (0, 1):
-            p = 2 * j + odd
-            _, rel_copy, drt_copy, com_copy, x_copy = sends(p, odd)
-            x_copy().wait_recv()
-            cols = pl.ds(pl.multiple_of(p * wide, wide), wide)
-            out_ref[:, cols] = (acc[p] + x_in[p].astype(F32)).astype(BF16)
-            rel_copy().wait_send()
-            drt_copy().wait_send()
-            com_copy().wait_send()
-            x_copy().wait_send()
-        return carry
-
-    lax.fori_loop(0, PIECES // 2, finish, 0)
+
+    def columns(p):
+        return pl.ds(pl.multiple_of(p * wide, wide), wide)
+
+    def multiply(p):
+        product = jnp.dot(g2[...], w2[:, columns(p)], preferred_element_type=F32)
+        part[p] = product.astype(BF16).reshape(2, half, wide)
+
+    def stage(x_step, y_step):
+        def both(k, carry):
+            x_step(k)
+            y_step(k)
+            return carry
+
+        def one(k, carry):
+            (x_step if n_x > n_y else y_step)(k)
+            return carry
+
+        lax.fori_loop(0, min(n_x, n_y), both, 0)
+        lax.fori_loop(min(n_x, n_y), max(n_x, n_y), one, 0)
+
+    def x_start(k):
+        multiply(k)
+        x_first(k)[4]().start()
+
+    def y_start(k):
+        multiply(n_x + k)
+        _, _, rel, drt, _, _ = y_first(k)
+        rel().start()
+        drt().start()
+
+    stage(x_start, y_start)
+
+    def x_second(k):
+        _, rel, drt, _, cross = x_first(k)
+        cross().wait_recv()
+        part[k, 0] = (part[k, 0].astype(F32) + x_in[k].astype(F32)).astype(BF16)
+        rel().start()
+        drt().start()
+
+    def y_second(k):
+        p, near, rel, _, com, _ = y_first(k)
+        rel().wait_recv()
+        part[p, :, block(near)] = (part[p, :, block(near)].astype(F32) + y_rel[k].astype(F32)).astype(BF16)
+        com().start()
+
+    stage(x_second, y_second)
+
+    def x_third(k):
+        near, rel, _, com, _ = x_first(k)
+        rel().wait_recv()
+        part[k, 0, block(near)] = (part[k, 0, block(near)].astype(F32) + x_rel[k].astype(F32)).astype(BF16)
+        com().start()
+
+    def y_third(k):
+        p, _, _, drt, com, cross = y_first(k)
+        drt().wait_recv()
+        com().wait_recv()
+        total = part[p, :, block(0)].astype(F32) + y_drt[k].astype(F32) + y_com[k].astype(F32)
+        y_out[k] = total[1].astype(BF16)
+        cross().start()
+        acc[k] = total[0]
+
+    stage(x_third, y_third)
+
+    def x_last(k):
+        _, rel, drt, com, cross = x_first(k)
+        drt().wait_recv()
+        com().wait_recv()
+        total = part[k, 0, block(0)].astype(F32) + x_drt[k].astype(F32) + x_com[k].astype(F32)
+        out_ref[:, columns(k)] = total.astype(BF16)
+        for copy in (rel, drt, com, cross):
+            copy().wait_send()
+
+    def y_last(k):
+        p, _, rel, drt, com, cross = y_first(k)
+        cross().wait_recv()
+        out_ref[:, columns(p)] = (acc[k] + y_in[k].astype(F32)).astype(BF16)
+        for copy in (rel, drt, com, cross):
+            copy().wait_send()
+
+    stage(x_last, y_last)
     for copy in state_copies:
         copy.wait_send()
     w_copy.wait_send()
@@ -291,17 +334,20 @@
     modes = residues.shape[1]
     width = out_weight.shape[1]
     rows = tokens // n_tp
-    wide = width // PIECES
+    wide = width // (X_PIECES + Y_PIECES)
     groups = chans // LANES
-    any_space = pl.BlockSpec(memory_space=pl.ANY)
+    hbm = pl.BlockSpec(memory_space=pltpu.HBM)
     vmem = pl.BlockSpec(memory_space=pltpu.VMEM)
     dma = pltpu.SemaphoreType.DMA
     return pl.pallas_call(
         kernel,
         out_shape=jax.ShapeDtypeStruct((rows, width), BF16),
-        in_specs=[any_space] * 3 + [vmem] * 3 + [any_space],
+        in_specs=[hbm] * 7,
         out_specs=vmem,
         scratch_shapes=[
+            pltpu.VMEM((modes, chans), F32),
+            pltpu.VMEM((modes, chans), F32),
+            pltpu.VMEM((1, chans), F32),
             pltpu.VMEM((tokens, chans), BF16),
             pltpu.VMEM((tokens, chans), BF16),
             pltpu.VMEM((tokens, chans), BF16),
@@ -312,25 +358,27 @@
             pltpu.VMEM((n_ctx, modes, chans), F32),
             pltpu.VMEM((tokens // 2, chans), BF16),
             pltpu.VMEM((tokens // 2, 2 * chans), BF16),
-            pltpu.VMEM((PIECES, tokens // 2, wide), BF16),
-            pltpu.VMEM((PIECES, 2 * rows, wide), BF16),
-            pltpu.VMEM((PIECES, 2 * rows, wide), BF16),
-            pltpu.VMEM((PIECES, 2 * rows, wide), BF16),
-            pltpu.VMEM((PIECES, rows, wide), BF16),
-            pltpu.VMEM((PIECES, rows, wide), BF16),
-            pltpu.VMEM((PIECES, rows, wide), F32),
-            dma((4,)),
+            pltpu.VMEM((X_PIECES + Y_PIECES, 2, YS * rows, wide), BF16),
+            pltpu.VMEM((X_PIECES, YS * rows, wide), BF16),
+            pltpu.VMEM((X_PIECES, rows, wide), BF16),
+            pltpu.VMEM((X_PIECES, rows, wide), BF16),
+            pltpu.VMEM((X_PIECES, rows, wide), BF16),
+            pltpu.VMEM((Y_PIECES, 2, rows, wide), BF16),
+            pltpu.VMEM((Y_PIECES, 2, rows, wide), BF16),
+            pltpu.VMEM((Y_PIECES, 2, rows, wide), BF16),
+            pltpu.VMEM((Y_PIECES, rows, wide), BF16),
+            pltpu.VMEM((Y_PIECES, rows, wide), BF16),
+            pltpu.VMEM((Y_PIECES, rows, wide), F32),
+            dma((7,)),
             dma((n_ctx - 1,)),
             dma((n_ctx - 1,)),
             dma((2,)),
             dma((2,)),
-            dma((2, PIECES)),
-            dma((2, PIECES)),
-            dma((2, PIECES)),
-            dma((2, PIECES)),
+            dma((4, 2, X_PIECES)),
+            dma((4, 2, Y_PIECES)),
         ],
         compiler_params=pltpu.CompilerParams(
-            collective_id=0, has_side_effects=True, vmem_limit_bytes=48 * 1024 * 1024
+            collective_id=0, has_side_effects=True, vmem_limit_bytes=62 * 1024 * 1024
         ),
         cost_estimate=pl.CostEstimate(
             flops=2 * tokens * chans * width, bytes_accessed=4 * 1024 * 1024, transcendentals=0

time: 45.9 us -> 36.9 us (0.80)
  local copies, waits for them, and re-layouts: 7.26 us -> 1.67 us
  Pallas kernels: 38.3 us -> 34.7 us
    unnamed x15 -> x1, local copies, waits for them, and re-layouts: 7.26 us -> 1.67 us
    pallas_call x1, Pallas kernels: 38.3 us -> 34.7 us  [body(): pl.pallas_call(kernel, out_shape=jax.ShapeDtypeStruct((rows, width), BF16...]
where the time goes in v2:
time: 36.9 us; the launch traced here: 36.4 us
  Pallas kernels  34.7 us (94%)
  local copies, waits for them, and re-layouts  1.67 us (5%)
    pallas_call x1, Pallas kernels, body(): pl.pallas_call(kernel, out_shape=jax.ShapeDtypeStruct((rows, width), BF16...  34.7 us
    unnamed x1, local copies, waits for them, and re-layouts  1.67 us

profile of v2, /device:TPU:1, one launch (start us, length us, event | category | flops | bytes accessed | tf_op | source)
XLA Modules:
  0.0 36.4 jit_solution(5560907306401401399)
XLA Ops:
  0.0 34.7 %shard_map.73 = bf16[32,4096]{1,0:T(8,128)(2,1)} custom-call(bf16[512,256]{1,0:T(8,128)(2,1)} %in_hbm.1, bf16[512,256]{1,0:T(8,128)(2,1)} %val_hbm.1, bf16[512,256]{1,0:T(8,128)(2,1)} %gate_hbm.1, f32[16,256]{1,0:T(8,128)} %bitcast.3, f32[16,256]{1,0:T(8,128)} %bitcast.4, f32[1,256]{1,0:T(1,128)} %bitcast.5, bf16[256,4096]{1,0:T(8,128)(2,1)} %w_hbm.1), custom_call_target="tpu_custom_call" | custom-call | flops 1073741824 | bytes 4194304 | tf_op jit(solution)/shard_map/pallas_call | solution.py:342
  34.7 1.7 %copy.9 = bf16[32,4096]{1,0:T(8,128)(2,1)} copy(bf16[32,4096]{1,0:T(8,128)(2,1)} %shard_map.73) | data formatting | bytes 524288

commit v3 on v2

--- a/solution.py
+++ b/solution.py
@@ -15,6 +15,8 @@
 SUB = 8
 YS = 4
 X_PIECES, Y_PIECES = 7, 9
+
+SCHEDULE = (('y', 0, 0), ('x', 0, 0), ('y', 1, 0), ('x', 1, 0), ('y', 2, 0), ('x', 2, 0), ('y', 3, 0), ('x', 3, 0), ('y', 4, 0), ('x', 4, 0), ('y', 5, 0), ('d', 5, 0), ('y', 6, 0), ('d', 6, 0), ('y', 7, 0), ('y', 8, 0), ('y', 0, 1), ('y', 1, 1), ('x', 0, 1), ('y', 2, 1), ('y', 3, 1), ('x', 1, 1), ('y', 4, 1), ('y', 5, 1), ('x', 2, 1), ('y', 6, 1), ('y', 7, 1), ('x', 3, 1), ('y', 8, 1), ('y', 0, 2), ('x', 4, 1), ('y', 1, 2), ('x', 0, 2), ('y', 2, 2), ('y', 3, 2), ('x', 1, 2), ('d', 5, 1), ('y', 4, 2), ('y', 5, 2), ('x', 2, 2), ('d', 6, 1), ('y', 6, 2), ('y', 0, 3), ('y', 7, 2), ('x', 3, 2), ('y', 1, 3), ('x', 4, 2), ('y', 2, 3), ('x', 0, 3), ('y', 3, 3), ('y', 8, 2), ('y', 4, 3), ('x', 1, 3), ('y', 5, 3), ('x', 2, 3), ('d', 5, 2), ('y', 6, 3), ('y', 7, 3), ('d', 6, 2), ('x', 4, 3), ('x', 3, 3), ('y', 8, 3))
 
 
 def kernel(
@@ -44,10 +46,11 @@
     up = device(ctx, xh, lax.rem(y + 1, YS), core)
     down = device(ctx, xh, lax.rem(y + YS - 1, YS), core)
     across = device(ctx, 1 - xh, y, core)
+    far = device(ctx, xh, lax.rem(y + 2, YS), core)
     others = [(lax.rem(ctx + k, n_ctx), tp) for k in range(1, n_ctx)]
 
     barrier = pltpu.get_barrier_semaphore()
-    peers = [partner, up, down, across] + others
+    peers = [partner, up, down, far, across] + others
     for peer in peers:
         pl.semaphore_signal(barrier, inc=1, device_id=peer, device_id_type=MESH)
 
@@ -116,12 +119,17 @@
         )
         copy.start()
         state_copies.append(copy)
-    w_copy = pltpu.make_async_remote_copy(
-        src_ref=w_hbm, dst_ref=w2.at[pl.ds(chans, chans)],
-        send_sem=pair_send.at[0], recv_sem=pair_recv.at[0],
-        device_id=partner, device_id_type=MESH,
-    )
-    w_copy.start()
+    w_copies = [
+        pltpu.make_async_remote_copy(
+            src_ref=w_hbm.at[pl.ds(h * chans // 2, chans // 2)],
+            dst_ref=w2.at[pl.ds(chans + h * chans // 2, chans // 2)],
+            send_sem=pair_send.at[groups + h], recv_sem=pair_recv.at[groups + h],
+            device_id=partner, device_id_type=MESH,
+        )
+        for h in range(2)
+    ]
+    for copy in w_copies:
+        copy.start()
 
     for g in range(groups):
         lanes = pl.ds(g * LANES, LANES)
@@ -145,6 +153,19 @@
     for copy in state_copies:
         copy.wait_recv()
 
+    loads[2].wait()
+
+    def target_block(r, q, core_i):
+        xh_t = lax.rem(xh + q, 2)
+        return (xh_t * YS + lax.rem(y + r, YS)) * 2 + core_i
+
+    def gated_rows(block, g):
+        at = pl.ds(pl.multiple_of(block * rows, rows), rows)
+        lanes = pl.ds(g * LANES, LANES)
+        gate = og[at, lanes].astype(F32)
+        return (gate * (py[g, at, :] + skip_ref[:, lanes] * px[g, at, :])).astype(BF16)
+
+    g_copies = []
     for g in range(groups):
         lanes = pl.ds(g * LANES, LANES)
         decay, step_factor = group_decay(g)
@@ -169,40 +190,25 @@
             return tuple(f * v for f, v in zip(factors, fades))
 
         lax.fori_loop(0, steps, extend, fades, unroll=4)
-
-    loads[2].wait()
-
-    def gated_rows(block, g):
-        at = pl.ds(pl.multiple_of(block * rows, rows), rows)
-        lanes = pl.ds(g * LANES, LANES)
-        gate = og[at, lanes].astype(F32)
-        return (gate * (py[g, at, :] + skip_ref[:, lanes] * px[g, at, :])).astype(BF16)
-
-    def target_block(r, q, core_i):
-        xh_t = lax.rem(xh + q, 2)
-        return (xh_t * YS + lax.rem(y + r, YS)) * 2 + core_i
-
-    for r in range(YS):
-        for q in range(2):
-            for g in range(groups):
-                g_out[pl.ds((q * YS + r) * rows, rows), pl.ds(g * LANES, LANES)] = gated_rows(
-                    target_block(r, q, 1 - core), g
-                )
-    g_copy = pltpu.make_async_remote_copy(
-        src_ref=g_out, dst_ref=g2.at[:, pl.ds(chans, chans)],
-        send_sem=pair_send.at[1], recv_sem=pair_recv.at[1],
-        device_id=partner, device_id_type=MESH,
-    )
-    g_copy.start()
-    for r in range(YS):
-        for q in range(2):
-            for g in range(groups):
+        for r in range(YS):
+            for q in range(2):
+                g_out[g, pl.ds((q * YS + r) * rows, rows), :] = gated_rows(target_block(r, q, 1 - core), g)
+        g_copy = pltpu.make_async_remote_copy(
+            src_ref=g_out.at[g], dst_ref=g2.at[:, pl.ds(chans + g * LANES, LANES)],
+            send_sem=pair_send.at[g], recv_sem=pair_recv.at[g],
+            device_id=partner, device_id_type=MESH,
+        )
+        g_copy.start()
+        g_copies.append(g_copy)
+    for g in range(groups):
+        for r in range(YS):
+            for q in range(2):
                 g2[pl.ds((q * YS + r) * rows, rows), pl.ds(g * LANES, LANES)] = gated_rows(
                     target_block(r, q, core), g
                 )
     loads[3].wait()
-    w_copy.wait_recv()
-    g_copy.wait_recv()
+    for copy in w_copies + g_copies:
+        copy.wait_recv()
 
     half = YS * rows
     n_x, n_y = x_in.shape[0], y_in.shape[0]
@@ -220,7 +226,7 @@
         return pl.ds(r * rows, rows)
 
     def y_first(k):
-        turn = lax.rem(k, 2)
+        turn = k % 2
         p = n_x + k
         src = part.at[p]
         return (
@@ -232,7 +238,7 @@
         )
 
     def x_first(k):
-        turn = lax.rem(k + 1, 2)
+        turn = (k + 1) % 2
         src = part.at[k, 0]
         return (
             1 + 2 * turn,
@@ -242,25 +248,15 @@
             functools.partial(send, part.at[k, 1], x_in.at[k], x_sem.at[3], k, across),
         )
 
+    def x_far(k):
+        return send(part.at[k, 0, block(2)], x_rel.at[k], x_sem.at[0], k, far)
+
     def columns(p):
-        return pl.ds(pl.multiple_of(p * wide, wide), wide)
+        return pl.ds(p * wide, wide)
 
     def multiply(p):
         product = jnp.dot(g2[...], w2[:, columns(p)], preferred_element_type=F32)
         part[p] = product.astype(BF16).reshape(2, half, wide)
-
-    def stage(x_step, y_step):
-        def both(k, carry):
-            x_step(k)
-            y_step(k)
-            return carry
-
-        def one(k, carry):
-            (x_step if n_x > n_y else y_step)(k)
-            return carry
-
-        lax.fori_loop(0, min(n_x, n_y), both, 0)
-        lax.fori_loop(min(n_x, n_y), max(n_x, n_y), one, 0)
 
     def x_start(k):
         multiply(k)
@@ -272,7 +268,6 @@
         rel().start()
         drt().start()
 
-    stage(x_start, y_start)
 
     def x_second(k):
         _, rel, drt, _, cross = x_first(k)
@@ -287,7 +282,26 @@
         part[p, :, block(near)] = (part[p, :, block(near)].astype(F32) + y_rel[k].astype(F32)).astype(BF16)
         com().start()
 
-    stage(x_second, y_second)
+
+    def x_second_direct(k):
+        _, _, drt, com, cross = x_first(k)
+        cross().wait_recv()
+        part[k, 0] = (part[k, 0].astype(F32) + x_in[k].astype(F32)).astype(BF16)
+        x_far(k).start()
+        drt().start()
+        com().start()
+
+    def x_last_direct(k):
+        _, _, drt, com, cross = x_first(k)
+        for copy in (x_far(k), drt(), com()):
+            copy.wait_recv()
+        summed = (
+            part[k, 0, block(0)].astype(F32) + x_drt[k].astype(F32)
+            + x_com[k].astype(F32) + x_rel[k].astype(F32)
+        )
+        out_ref[:, columns(k)] = summed.astype(BF16)
+        for copy in (x_far(k), drt(), com(), cross()):
+            copy.wait_send()
 
     def x_third(k):
         near, rel, _, com, _ = x_first(k)
@@ -299,19 +313,18 @@
         p, _, _, drt, com, cross = y_first(k)
         drt().wait_recv()
         com().wait_recv()
-        total = part[p, :, block(0)].astype(F32) + y_drt[k].astype(F32) + y_com[k].astype(F32)
-        y_out[k] = total[1].astype(BF16)
+        summed = part[p, :, block(0)].astype(F32) + y_drt[k].astype(F32) + y_com[k].astype(F32)
+        y_out[k] = summed[1].astype(BF16)
         cross().start()
-        acc[k] = total[0]
-
-    stage(x_third, y_third)
+        acc[k] = summed[0]
+
 
     def x_last(k):
         _, rel, drt, com, cross = x_first(k)
         drt().wait_recv()
         com().wait_recv()
-        total = part[k, 0, block(0)].astype(F32) + x_drt[k].astype(F32) + x_com[k].astype(F32)
-        out_ref[:, columns(k)] = total.astype(BF16)
+        summed = part[k, 0, block(0)].astype(F32) + x_drt[k].astype(F32) + x_com[k].astype(F32)
+        out_ref[:, columns(k)] = summed.astype(BF16)
         for copy in (rel, drt, com, cross):
             copy().wait_send()
 
@@ -322,11 +335,15 @@
         for copy in (rel, drt, com, cross):
             copy().wait_send()
 
-    stage(x_last, y_last)
-    for copy in state_copies:
+    steps_of = {
+        "x": (x_start, x_second, x_third, x_last),
+        "d": (x_start, x_second_direct, x_last_direct),
+        "y": (y_start, y_second, y_third, y_last),
+    }
+    for axis, k, stage in SCHEDULE:
+        steps_of[axis][stage](k)
+    for copy in state_copies + w_copies + g_copies:
         copy.wait_send()
-    w_copy.wait_send()
-    g_copy.wait_send()
 
 
 def body(n_ctx, n_tp, in_gate, value_stream, out_gate, residues, decays, skip_gain, out_weight):
@@ -341,7 +358,7 @@
     dma = pltpu.SemaphoreType.DMA
     return pl.pallas_call(
         kernel,
-        out_shape=jax.ShapeDtypeStruct((rows, width), BF16),
+        out_shape=pltpu.VMEM((rows, width), BF16),
         in_specs=[hbm] * 7,
         out_specs=vmem,
         scratch_shapes=[
@@ -356,7 +373,7 @@
             pltpu.VMEM((groups, tokens, LANES), F32),
             pltpu.VMEM((groups, modes, SUB, LANES), F32),
             pltpu.VMEM((n_ctx, modes, chans), F32),
-            pltpu.VMEM((tokens // 2, chans), BF16),
+            pltpu.VMEM((groups, tokens // 2, LANES), BF16),
             pltpu.VMEM((tokens // 2, 2 * chans), BF16),
             pltpu.VMEM((X_PIECES + Y_PIECES, 2, YS * rows, wide), BF16),
             pltpu.VMEM((X_PIECES, YS * rows, wide), BF16),
@@ -372,20 +389,24 @@
             dma((7,)),
             dma((n_ctx - 1,)),
             dma((n_ctx - 1,)),
-            dma((2,)),
-            dma((2,)),
+            dma((groups + 2,)),
+            dma((groups + 2,)),
             dma((4, 2, X_PIECES)),
             dma((4, 2, Y_PIECES)),
         ],
         compiler_params=pltpu.CompilerParams(
-            collective_id=0, has_side_effects=True, vmem_limit_bytes=62 * 1024 * 1024
+            collective_id=0, has_side_effects=True, vmem_limit_bytes=48 * 1024 * 1024
         ),
         cost_estimate=pl.CostEstimate(
             flops=2 * tokens * chans * width, bytes_accessed=4 * 1024 * 1024, transcendentals=0
         ),
     )(
-        in_gate, value_stream, out_gate, residues.T, decays.T,
-        skip_gain.reshape(1, chans), out_weight,
+        *(
+            pltpu.with_memory_space_constraint(operand, pltpu.HBM)
+            for operand in (
+                in_gate, value_stream, out_gate, residues.T, decays.T, skip_gain.reshape(1, chans), out_weight
+            )
+        )
     )
 
 

time: 36.9 us -> 33.4 us (0.905); the launches traced: 36.4 us -> 33.3 us
  Pallas kernels: 34.7 us -> 32.6 us
  local copies, waits for them, and re-layouts: 1.67 us -> 0.71 us
    pallas_call x1, Pallas kernels: 34.7 us -> 32.6 us  [body(): pl.pallas_call(kernel, out_shape=pltpu.VMEM((rows, width), BF16), in_spec...]
    unnamed x1, local copies, waits for them, and re-layouts: 1.67 us -> 0.71 us
where the time goes in v3:
time: 33.4 us; the launch traced here: 33.3 us
  Pallas kernels  32.6 us (98%)
  local copies, waits for them, and re-layouts  0.71 us (2%)
    pallas_call x1, Pallas kernels, body(): pl.pallas_call(kernel, out_shape=pltpu.VMEM((rows, width), BF16), in_spec...  32.6 us
    unnamed x1, local copies, waits for them, and re-layouts  0.71 us

profile of v3, /device:TPU:1, one launch (start us, length us, event | category | flops | bytes accessed | tf_op | source)
XLA Modules:
  0.0 33.3 jit_solution(7122715224705252529)
XLA Ops:
  0.0 32.6 %shard_map.73 = bf16[32,4096]{1,0:T(8,128)(2,1)S(1)} custom-call(bf16[512,256]{1,0:T(8,128)(2,1)} %in_hbm.1, bf16[512,256]{1,0:T(8,128)(2,1)} %val_hbm.1, bf16[512,256]{1,0:T(8,128)(2,1)} %gate_hbm.1, f32[16,256]{1,0:T(8,128)} %bitcast.3, f32[16,256]{1,0:T(8,128)} %bitcast.4, f32[1,256]{1,0:T(1,128)} %bitcast.5, bf16[256,4096]{1,0:T(8,128)(2,1)} %w_hbm.1), custom_call_target="tpu_custom_call" | custom-call | flops 1073741824 | bytes 4194304 | tf_op jit(solution)/shard_map/pallas_call | solution.py:359
  32.6 0.7 %copy.9 = bf16[32,4096]{1,0:T(8,128)(2,1)} copy(bf16[32,4096]{1,0:T(8,128)(2,1)S(1)} %shard_map.73) | data formatting | bytes 524288

commit v4 on v3

--- a/solution.py
+++ b/solution.py
@@ -47,12 +47,6 @@
     down = device(ctx, xh, lax.rem(y + YS - 1, YS), core)
     across = device(ctx, 1 - xh, y, core)
     far = device(ctx, xh, lax.rem(y + 2, YS), core)
-    others = [(lax.rem(ctx + k, n_ctx), tp) for k in range(1, n_ctx)]
-
-    barrier = pltpu.get_barrier_semaphore()
-    peers = [partner, up, down, far, across] + others
-    for peer in peers:
-        pl.semaphore_signal(barrier, inc=1, device_id=peer, device_id_type=MESH)
 
     small = [
         pltpu.make_async_copy(dec_hbm, dec_ref, load_sem.at[4]),
@@ -65,10 +59,22 @@
         pltpu.make_async_copy(gate_hbm, og, load_sem.at[2]),
         pltpu.make_async_copy(w_hbm, w2.at[pl.ds(0, chans)], load_sem.at[3]),
     ]
-    for load in loads[:2] + small + loads[2:]:
+    for load in loads[:2] + small:
         load.start()
+    barrier = pltpu.get_barrier_semaphore()
+    peers = [partner, up, down, far, across]
+    for peer in peers:
+        pl.semaphore_signal(barrier, inc=1, device_id=peer, device_id_type=MESH)
+    for k in range(1, n_ctx):
+
+        @pl.when(ctx >= k)
+        def _(k=k):
+            pl.semaphore_signal(barrier, inc=1, device_id=(ctx - k, tp), device_id_type=MESH)
+
     loads[0].wait()
     loads[1].wait()
+    for load in loads[2:]:
+        load.start()
 
     for g in range(groups):
         lanes = pl.ds(g * LANES, LANES)
@@ -109,16 +115,21 @@
                 scan = scan + weight * pltpu.roll(scan, hop, 0)
             prefix[g, m] = scan
 
-    pl.semaphore_wait(barrier, len(peers))
-    state_copies = []
-    for k, peer in enumerate(others):
-        copy = pltpu.make_async_remote_copy(
+    pl.semaphore_wait(barrier, len(peers) + n_ctx - 1 - ctx)
+
+    def state_copy(k):
+        return pltpu.make_async_remote_copy(
             src_ref=states.at[ctx], dst_ref=states.at[ctx],
-            send_sem=st_send.at[k], recv_sem=st_recv.at[k],
-            device_id=peer, device_id_type=MESH,
-        )
-        copy.start()
-        state_copies.append(copy)
+            send_sem=st_send.at[k - 1], recv_sem=st_recv.at[k - 1],
+            device_id=(lax.rem(ctx + k, n_ctx), tp), device_id_type=MESH,
+        )
+
+    for k in range(1, n_ctx):
+
+        @pl.when(ctx + k < n_ctx)
+        def _(k=k):
+            state_copy(k).start()
+
     w_copies = [
         pltpu.make_async_remote_copy(
             src_ref=w_hbm.at[pl.ds(h * chans // 2, chans // 2)],
@@ -150,8 +161,12 @@
 
         lax.fori_loop(0, steps, convolve, tuple(prefix[g, m] for m in range(modes)), unroll=4)
 
-    for copy in state_copies:
-        copy.wait_recv()
+    for k in range(1, n_ctx):
+
+        @pl.when(ctx >= k)
+        def _(k=k):
+            state_copy(k).wait_recv()
+
 
     loads[2].wait()
 
@@ -165,31 +180,41 @@
         gate = og[at, lanes].astype(F32)
         return (gate * (py[g, at, :] + skip_ref[:, lanes] * px[g, at, :])).astype(BF16)
 
-    g_copies = []
-    for g in range(groups):
+    def carry_in(g):
         lanes = pl.ds(g * LANES, LANES)
         decay, step_factor = group_decay(g)
         amplitude = res_ref[:, lanes] * jnp.sqrt(2.0 * decay)
         block_factor = jnp.exp(-decay * float(tokens))
-        carried = jnp.zeros((modes, LANES), F32)
-        for i in range(n_ctx - 1):
-            carried = jnp.where(i < ctx, block_factor * carried + states[i, :, lanes], carried)
-        carried = carried * amplitude
+
+        def collect(i, carried):
+            return block_factor * carried + states[i, :, lanes]
+
+        return lax.fori_loop(0, ctx, collect, jnp.zeros((modes, LANES), F32)) * amplitude
+
+    def extend_rows(g, carried, owner):
+        decay, step_factor = group_decay(g)
+        first = owner * rows
         factors = [spread(step_factor[m : m + 1]) for m in range(modes)]
+        ahead = place * steps + (first + 1).astype(F32)
         fades = tuple(
-            spread(carried[m : m + 1]) * jnp.exp(-spread(decay[m : m + 1]) * (place * steps + 1.0))
-            for m in range(modes)
-        )
-
-        def extend(i, fades, factors=factors, g=g):
-            rows_i = pl.ds(i, SUB, stride=steps)
+            spread(carried[m : m + 1]) * jnp.exp(-spread(decay[m : m + 1]) * ahead) for m in range(modes)
+        )
+
+        def extend(i, fades):
+            rows_i = pl.ds(first + i, SUB, stride=steps)
             terms = list(fades)
             while len(terms) > 1:
                 terms = [terms[j] + terms[j + 1] for j in range(0, len(terms), 2)]
             py[g, rows_i, :] = py[g, rows_i, :] + terms[0]
             return tuple(f * v for f, v in zip(factors, fades))
 
-        lax.fori_loop(0, steps, extend, fades, unroll=4)
+        lax.fori_loop(0, rows, extend, fades, unroll=4)
+
+    g_copies = []
+    carries = []
+    for g in range(groups):
+        carries.append(carry_in(g))
+        extend_rows(g, carries[g], 1 - core)
         for r in range(YS):
             for q in range(2):
                 g_out[g, pl.ds((q * YS + r) * rows, rows), :] = gated_rows(target_block(r, q, 1 - core), g)
@@ -201,6 +226,7 @@
         g_copy.start()
         g_copies.append(g_copy)
     for g in range(groups):
+        extend_rows(g, carries[g], core)
         for r in range(YS):
             for q in range(2):
                 g2[pl.ds((q * YS + r) * rows, rows), pl.ds(g * LANES, LANES)] = gated_rows(
@@ -342,7 +368,13 @@
     }
     for axis, k, stage in SCHEDULE:
         steps_of[axis][stage](k)
-    for copy in state_copies + w_copies + g_copies:
+    for k in range(1, n_ctx):
+
+        @pl.when(ctx + k < n_ctx)
+        def _(k=k):
+            state_copy(k).wait_send()
+
+    for copy in w_copies + g_copies:
         copy.wait_send()
 
 

time: 33.4 us -> 32.2 us (0.964); the launches traced: 33.3 us -> 31.7 us
  Pallas kernels: 32.6 us -> 30.9 us
    pallas_call x1, Pallas kernels: 32.6 us -> 30.9 us  [body(): pl.pallas_call(kernel, out_shape=pltpu.VMEM((rows, width), BF16), in_spec...]
where the time goes in v4:
time: 32.2 us; the launch traced here: 31.7 us
  Pallas kernels  30.9 us (96%)
  local copies, waits for them, and re-layouts  0.71 us (2%)
    pallas_call x1, Pallas kernels, body(): pl.pallas_call(kernel, out_shape=pltpu.VMEM((rows, width), BF16), in_spec...  30.9 us
    unnamed x1, local copies, waits for them, and re-layouts  0.71 us

profile of v4, /device:TPU:1, one launch (start us, length us, event | category | flops | bytes accessed | tf_op | source)
XLA Modules:
  0.0 31.7 jit_solution(1192698210733059940)
XLA Ops:
  0.0 30.9 %shard_map.73 = bf16[32,4096]{1,0:T(8,128)(2,1)S(1)} custom-call(bf16[512,256]{1,0:T(8,128)(2,1)} %in_hbm.1, bf16[512,256]{1,0:T(8,128)(2,1)} %val_hbm.1, bf16[512,256]{1,0:T(8,128)(2,1)} %gate_hbm.1, f32[16,256]{1,0:T(8,128)} %bitcast.3, f32[16,256]{1,0:T(8,128)} %bitcast.4, f32[1,256]{1,0:T(1,128)} %bitcast.5, bf16[256,4096]{1,0:T(8,128)(2,1)} %w_hbm.1), custom_call_target="tpu_custom_call" | custom-call | flops 1073741824 | bytes 4194304 | tf_op jit(solution)/shard_map/pallas_call | solution.py:391
  31.0 0.7 %copy.9 = bf16[32,4096]{1,0:T(8,128)(2,1)} copy(bf16[32,4096]{1,0:T(8,128)(2,1)S(1)} %shard_map.73) | data formatting | bytes 524288

commit v5 on v4

--- a/solution.py
+++ b/solution.py
@@ -14,6 +14,7 @@
 LANES = 128
 SUB = 8
 YS = 4
+W_CHUNKS = 4
 X_PIECES, Y_PIECES = 7, 9
 
 SCHEDULE = (('y', 0, 0), ('x', 0, 0), ('y', 1, 0), ('x', 1, 0), ('y', 2, 0), ('x', 2, 0), ('y', 3, 0), ('x', 3, 0), ('y', 4, 0), ('x', 4, 0), ('y', 5, 0), ('d', 5, 0), ('y', 6, 0), ('d', 6, 0), ('y', 7, 0), ('y', 8, 0), ('y', 0, 1), ('y', 1, 1), ('x', 0, 1), ('y', 2, 1), ('y', 3, 1), ('x', 1, 1), ('y', 4, 1), ('y', 5, 1), ('x', 2, 1), ('y', 6, 1), ('y', 7, 1), ('x', 3, 1), ('y', 8, 1), ('y', 0, 2), ('x', 4, 1), ('y', 1, 2), ('x', 0, 2), ('y', 2, 2), ('y', 3, 2), ('x', 1, 2), ('d', 5, 1), ('y', 4, 2), ('y', 5, 2), ('x', 2, 2), ('d', 6, 1), ('y', 6, 2), ('y', 0, 3), ('y', 7, 2), ('x', 3, 2), ('y', 1, 3), ('x', 4, 2), ('y', 2, 3), ('x', 0, 3), ('y', 3, 3), ('y', 8, 2), ('y', 4, 3), ('x', 1, 3), ('y', 5, 3), ('x', 2, 3), ('d', 5, 2), ('y', 6, 3), ('y', 7, 3), ('d', 6, 2), ('x', 4, 3), ('x', 3, 3), ('y', 8, 3))
@@ -22,8 +23,8 @@
 def kernel(
     in_hbm, val_hbm, gate_hbm, res_hbm, dec_hbm, skip_hbm, w_hbm, out_ref,
     res_ref, dec_ref, skip_ref, ig, vs, og, w2, px, py, prefix, states, g_out, g2, part,
-    x_in, x_rel, x_drt, x_com, y_rel, y_drt, y_com, y_out, y_in, acc,
-    load_sem, st_send, st_recv, pair_send, pair_recv, x_sem, y_sem,
+    x_in, x_rel, x_dc, y_rel, y_dc, y_out, y_in, acc,
+    load_sem, st_send, st_recv, pair_send, pair_recv, sent, x_sem, y_sem,
 ):
     tokens, chans = px.shape[1], px.shape[0] * LANES
     steps = tokens // SUB
@@ -130,16 +131,17 @@
         def _(k=k):
             state_copy(k).start()
 
+    chunk = w2.shape[1] // W_CHUNKS
     w_copies = [
         pltpu.make_async_remote_copy(
-            src_ref=w_hbm.at[pl.ds(h * chans // 2, chans // 2)],
-            dst_ref=w2.at[pl.ds(chans + h * chans // 2, chans // 2)],
-            send_sem=pair_send.at[groups + h], recv_sem=pair_recv.at[groups + h],
+            src_ref=w_hbm.at[:, pl.ds(c * chunk, chunk)],
+            dst_ref=w2.at[pl.ds(chans, chans), pl.ds(c * chunk, chunk)],
+            send_sem=pair_send.at[groups + c], recv_sem=pair_recv.at[groups + c],
             device_id=partner, device_id_type=MESH,
         )
-        for h in range(2)
+        for c in range(W_CHUNKS)
     ]
-    for copy in w_copies:
+    for copy in w_copies[: W_CHUNKS // 2]:
         copy.start()
 
     for g in range(groups):
@@ -225,6 +227,8 @@
         )
         g_copy.start()
         g_copies.append(g_copy)
+    for copy in w_copies[W_CHUNKS // 2 :]:
+        copy.start()
     for g in range(groups):
         extend_rows(g, carries[g], core)
         for r in range(YS):
@@ -233,17 +237,20 @@
                     target_block(r, q, core), g
                 )
     loads[3].wait()
-    for copy in w_copies + g_copies:
+    for copy in g_copies:
         copy.wait_recv()
 
     half = YS * rows
     n_x, n_y = x_in.shape[0], y_in.shape[0]
 
-    def send(src, dst, sems, k, to):
+    def send(src, dst, kind, sem, to):
         return pltpu.make_async_remote_copy(
-            src_ref=src, dst_ref=dst, send_sem=sems.at[0, k], recv_sem=sems.at[1, k],
+            src_ref=src, dst_ref=dst, send_sem=sent.at[kind], recv_sem=sem,
             device_id=to, device_id_type=MESH,
         )
+
+    def landed(dst, sem):
+        send(dst, dst, 0, sem, across).wait_recv()
 
     def neighbour(turn):
         return device(ctx, xh, lax.rem(y + 1 + 2 * turn, YS), core)
@@ -257,10 +264,10 @@
         src = part.at[p]
         return (
             p, 1 + 2 * turn,
-            functools.partial(send, src.at[:, block(2)], y_rel.at[k], y_sem.at[0], k, neighbour(turn)),
-            functools.partial(send, src.at[:, block(3 - 2 * turn)], y_drt.at[k], y_sem.at[1], k, neighbour(1 - turn)),
-            functools.partial(send, src.at[:, block(1 + 2 * turn)], y_com.at[k], y_sem.at[2], k, neighbour(turn)),
-            functools.partial(send, y_out.at[k], y_in.at[k], y_sem.at[3], k, across),
+            functools.partial(send, src.at[:, block(2)], y_rel.at[k], 0, y_sem.at[0, k], neighbour(turn)),
+            functools.partial(send, src.at[:, block(3 - 2 * turn)], y_dc.at[k, 0], 1, y_sem.at[1, k], neighbour(1 - turn)),
+            functools.partial(send, src.at[:, block(1 + 2 * turn)], y_dc.at[k, 1], 1, y_sem.at[1, k], neighbour(turn)),
+            functools.partial(send, y_out.at[k], y_in.at[k], 2, y_sem.at[2, k], across),
         )
 
     def x_first(k):
@@ -268,19 +275,24 @@
         src = part.at[k, 0]
         return (
             1 + 2 * turn,
-            functools.partial(send, src.at[block(2)], x_rel.at[k], x_sem.at[0], k, neighbour(turn)),
-            functools.partial(send, src.at[block(3 - 2 * turn)], x_drt.at[k], x_sem.at[1], k, neighbour(1 - turn)),
-            functools.partial(send, src.at[block(1 + 2 * turn)], x_com.at[k], x_sem.at[2], k, neighbour(turn)),
-            functools.partial(send, part.at[k, 1], x_in.at[k], x_sem.at[3], k, across),
+            functools.partial(send, src.at[block(2)], x_rel.at[k], 4, x_sem.at[1, k], neighbour(turn)),
+            functools.partial(send, src.at[block(3 - 2 * turn)], x_dc.at[k, 0], 5, x_sem.at[2, k], neighbour(1 - turn)),
+            functools.partial(send, src.at[block(1 + 2 * turn)], x_dc.at[k, 1], 5, x_sem.at[2, k], neighbour(turn)),
+            functools.partial(send, part.at[k, 1], x_in.at[k], 3, x_sem.at[0, k], across),
         )
 
     def x_far(k):
-        return send(part.at[k, 0, block(2)], x_rel.at[k], x_sem.at[0], k, far)
+        return send(part.at[k, 0, block(2)], x_rel.at[k], 4, x_sem.at[1, k], far)
+
+    started = [(axis == "y", k) for axis, k, stage in SCHEDULE if stage == 0]
 
     def columns(p):
-        return pl.ds(p * wide, wide)
+        return pl.ds(started.index((p >= n_x, p - n_x if p >= n_x else p)) * wide, wide)
 
     def multiply(p):
+        first = columns(p).start
+        if first % chunk == 0:
+            w_copies[first // chunk].wait_recv()
         product = jnp.dot(g2[...], w2[:, columns(p)], preferred_element_type=F32)
         part[p] = product.astype(BF16).reshape(2, half, wide)
 
@@ -319,15 +331,13 @@
 
     def x_last_direct(k):
         _, _, drt, com, cross = x_first(k)
-        for copy in (x_far(k), drt(), com()):
-            copy.wait_recv()
+        landed(x_rel.at[k], x_sem.at[1, k])
+        landed(x_dc.at[k], x_sem.at[2, k])
         summed = (
-            part[k, 0, block(0)].astype(F32) + x_drt[k].astype(F32)
-            + x_com[k].astype(F32) + x_rel[k].astype(F32)
+            part[k, 0, block(0)].astype(F32) + x_dc[k, 0].astype(F32)
+            + x_dc[k, 1].astype(F32) + x_rel[k].astype(F32)
         )
         out_ref[:, columns(k)] = summed.astype(BF16)
-        for copy in (x_far(k), drt(), com(), cross()):
-            copy.wait_send()
 
     def x_third(k):
         near, rel, _, com, _ = x_first(k)
@@ -337,9 +347,8 @@
 
     def y_third(k):
         p, _, _, drt, com, cross = y_first(k)
-        drt().wait_recv()
-        com().wait_recv()
-        summed = part[p, :, block(0)].astype(F32) + y_drt[k].astype(F32) + y_com[k].astype(F32)
+        landed(y_dc.at[k], y_sem.at[1, k])
+        summed = part[p, :, block(0)].astype(F32) + y_dc[k, 0].astype(F32) + y_dc[k, 1].astype(F32)
         y_out[k] = summed[1].astype(BF16)
         cross().start()
         acc[k] = summed[0]
@@ -347,19 +356,14 @@
 
     def x_last(k):
         _, rel, drt, com, cross = x_first(k)
-        drt().wait_recv()
-        com().wait_recv()
-        summed = part[k, 0, block(0)].astype(F32) + x_drt[k].astype(F32) + x_com[k].astype(F32)
+        landed(x_dc.at[k], x_sem.at[2, k])
+        summed = part[k, 0, block(0)].astype(F32) + x_dc[k, 0].astype(F32) + x_dc[k, 1].astype(F32)
         out_ref[:, columns(k)] = summed.astype(BF16)
-        for copy in (rel, drt, com, cross):
-            copy().wait_send()
 
     def y_last(k):
         p, _, rel, drt, com, cross = y_first(k)
         cross().wait_recv()
         out_ref[:, columns(p)] = (acc[k] + y_in[k].astype(F32)).astype(BF16)
-        for copy in (rel, drt, com, cross):
-            copy().wait_send()
 
     steps_of = {
         "x": (x_start, x_second, x_third, x_last),
@@ -376,6 +380,8 @@
 
     for copy in w_copies + g_copies:
         copy.wait_send()
+    for kind, whole in enumerate((y_rel, y_dc, y_in, x_in, x_rel, x_dc)):
+        send(whole, whole, kind, y_sem.at[0, 0], across).wait_send()
 
 
 def body(n_ctx, n_tp, in_gate, value_stream, out_gate, residues, decays, skip_gain, out_weight):
@@ -410,21 +416,20 @@
             pltpu.VMEM((X_PIECES + Y_PIECES, 2, YS * rows, wide), BF16),
             pltpu.VMEM((X_PIECES, YS * rows, wide), BF16),
             pltpu.VMEM((X_PIECES, rows, wide), BF16),
-            pltpu.VMEM((X_PIECES, rows, wide), BF16),
-            pltpu.VMEM((X_PIECES, rows, wide), BF16),
+            pltpu.VMEM((X_PIECES, 2, rows, wide), BF16),
             pltpu.VMEM((Y_PIECES, 2, rows, wide), BF16),
-            pltpu.VMEM((Y_PIECES, 2, rows, wide), BF16),
-            pltpu.VMEM((Y_PIECES, 2, rows, wide), BF16),
+            pltpu.VMEM((Y_PIECES, 2, 2, rows, wide), BF16),
             pltpu.VMEM((Y_PIECES, rows, wide), BF16),
             pltpu.VMEM((Y_PIECES, rows, wide), BF16),
             pltpu.VMEM((Y_PIECES, rows, wide), F32),
             dma((7,)),
             dma((n_ctx - 1,)),
             dma((n_ctx - 1,)),
-            dma((groups + 2,)),
-            dma((groups + 2,)),
-            dma((4, 2, X_PIECES)),
-            dma((4, 2, Y_PIECES)),
+            dma((groups + W_CHUNKS,)),
+            dma((groups + W_CHUNKS,)),
+            dma((6,)),
+            dma((3, X_PIECES)),
+            dma((3, Y_PIECES)),
         ],
         compiler_params=pltpu.CompilerParams(
             collective_id=0, has_side_effects=True, vmem_limit_bytes=48 * 1024 * 1024

time: 32.2 us -> 31.6 us (0.981)
  the two profiles are of different devices: /device:TPU:1 before, /device:TPU:2 now
where the time goes in v5:
time: 31.6 us; the launch traced here: 31.4 us
  Pallas kernels  30.7 us (97%)
  local copies, waits for them, and re-layouts  0.71 us (2%)
    pallas_call x1, Pallas kernels, body(): pl.pallas_call(kernel, out_shape=pltpu.VMEM((rows, width), BF16), in_spec...  30.7 us
    unnamed x1, local copies, waits for them, and re-layouts  0.71 us

profile of v5, /device:TPU:2, one launch (start us, length us, event | category | flops | bytes accessed | tf_op | source)
XLA Modules:
  0.0 31.4 jit_solution(11894506747109160788)
XLA Ops:
  0.0 30.7 %shard_map.73 = bf16[32,4096]{1,0:T(8,128)(2,1)S(1)} custom-call(bf16[512,256]{1,0:T(8,128)(2,1)} %in_hbm.1, bf16[512,256]{1,0:T(8,128)(2,1)} %val_hbm.1, bf16[512,256]{1,0:T(8,128)(2,1)} %gate_hbm.1, f32[16,256]{1,0:T(8,128)} %bitcast.3, f32[16,256]{1,0:T(8,128)} %bitcast.4, f32[1,256]{1,0:T(1,128)} %bitcast.5, bf16[256,4096]{1,0:T(8,128)(2,1)} %w_hbm.1), custom_call_target="tpu_custom_call" | custom-call | flops 1073741824 | bytes 4194304 | tf_op jit(solution)/shard_map/pallas_call | solution.py:397
  30.7 0.7 %copy.9 = bf16[32,4096]{1,0:T(8,128)(2,1)} copy(bf16[32,4096]{1,0:T(8,128)(2,1)S(1)} %shard_map.73) | data formatting | bytes 524288

commit v6 on v5

--- a/solution.py
+++ b/solution.py
@@ -17,12 +17,12 @@
 W_CHUNKS = 4
 X_PIECES, Y_PIECES = 7, 9
 
-SCHEDULE = (('y', 0, 0), ('x', 0, 0), ('y', 1, 0), ('x', 1, 0), ('y', 2, 0), ('x', 2, 0), ('y', 3, 0), ('x', 3, 0), ('y', 4, 0), ('x', 4, 0), ('y', 5, 0), ('d', 5, 0), ('y', 6, 0), ('d', 6, 0), ('y', 7, 0), ('y', 8, 0), ('y', 0, 1), ('y', 1, 1), ('x', 0, 1), ('y', 2, 1), ('y', 3, 1), ('x', 1, 1), ('y', 4, 1), ('y', 5, 1), ('x', 2, 1), ('y', 6, 1), ('y', 7, 1), ('x', 3, 1), ('y', 8, 1), ('y', 0, 2), ('x', 4, 1), ('y', 1, 2), ('x', 0, 2), ('y', 2, 2), ('y', 3, 2), ('x', 1, 2), ('d', 5, 1), ('y', 4, 2), ('y', 5, 2), ('x', 2, 2), ('d', 6, 1), ('y', 6, 2), ('y', 0, 3), ('y', 7, 2), ('x', 3, 2), ('y', 1, 3), ('x', 4, 2), ('y', 2, 3), ('x', 0, 3), ('y', 3, 3), ('y', 8, 2), ('y', 4, 3), ('x', 1, 3), ('y', 5, 3), ('x', 2, 3), ('d', 5, 2), ('y', 6, 3), ('y', 7, 3), ('d', 6, 2), ('x', 4, 3), ('x', 3, 3), ('y', 8, 3))
+SCHEDULE = (('y', 0, 0), ('y', 1, 0), ('x', 0, 0), ('y', 2, 0), ('x', 1, 0), ('y', 3, 0), ('x', 2, 0), ('y', 4, 0), ('x', 3, 0), ('y', 5, 0), ('d', 4, 0), ('y', 6, 0), ('d', 5, 0), ('y', 7, 0), ('d', 6, 0), ('y', 8, 0), ('y', 0, 1), ('y', 1, 1), ('x', 0, 1), ('y', 2, 1), ('y', 3, 1), ('x', 1, 1), ('y', 4, 1), ('y', 5, 1), ('x', 2, 1), ('y', 6, 1), ('y', 7, 1), ('x', 3, 1), ('y', 8, 1), ('y', 0, 2), ('y', 1, 2), ('d', 4, 1), ('x', 0, 2), ('y', 2, 2), ('y', 3, 2), ('x', 1, 2), ('d', 5, 1), ('y', 4, 2), ('y', 5, 2), ('x', 2, 2), ('d', 6, 1), ('y', 6, 2), ('y', 7, 2), ('y', 0, 3), ('x', 3, 2), ('y', 1, 3), ('y', 8, 2), ('y', 2, 3), ('x', 0, 3), ('y', 3, 3), ('d', 4, 2), ('x', 1, 3), ('y', 4, 3), ('x', 2, 3), ('y', 5, 3), ('d', 5, 2), ('y', 6, 3), ('d', 6, 2), ('y', 7, 3), ('x', 3, 3), ('y', 8, 3))
 
 
 def kernel(
     in_hbm, val_hbm, gate_hbm, res_hbm, dec_hbm, skip_hbm, w_hbm, out_ref,
-    res_ref, dec_ref, skip_ref, ig, vs, og, w2, px, py, prefix, states, g_out, g2, part,
+    res_ref, dec_ref, skip_ref, ig, vs, og, w2, px, py, prefix, states, coarse, fading, g_out, g2, part,
     x_in, x_rel, x_dc, y_rel, y_dc, y_out, y_in, acc,
     load_sem, st_send, st_recv, pair_send, pair_recv, sent, x_sem, y_sem,
 ):
@@ -127,7 +127,13 @@
 
     for k in range(1, n_ctx):
 
-        @pl.when(ctx + k < n_ctx)
+        @pl.when(ctx + k == n_ctx // 2)
+        def _(k=k):
+            state_copy(k).start()
+
+    for k in range(1, n_ctx):
+
+        @pl.when((ctx + k < n_ctx) & (ctx + k != n_ctx // 2))
         def _(k=k):
             state_copy(k).start()
 
@@ -163,6 +169,16 @@
 
         lax.fori_loop(0, steps, convolve, tuple(prefix[g, m] for m in range(modes)), unroll=4)
 
+    for g in range(groups):
+        lanes = pl.ds(g * LANES, LANES)
+        decay, _ = group_decay(g)
+        amplitude = res_ref[:, lanes] * jnp.sqrt(2.0 * decay)
+        coarse[:, lanes] = jnp.exp(-decay * float(tokens))
+        for owner in range(2):
+            ahead = place * steps + float(owner * rows + 1)
+            for m in range(modes):
+                fading[owner, g, m] = spread(amplitude[m : m + 1]) * jnp.exp(-spread(decay[m : m + 1]) * ahead)
+
     for k in range(1, n_ctx):
 
         @pl.when(ctx >= k)
@@ -184,23 +200,18 @@
 
     def carry_in(g):
         lanes = pl.ds(g * LANES, LANES)
-        decay, step_factor = group_decay(g)
-        amplitude = res_ref[:, lanes] * jnp.sqrt(2.0 * decay)
-        block_factor = jnp.exp(-decay * float(tokens))
+        block_factor = coarse[:, lanes]
 
         def collect(i, carried):
             return block_factor * carried + states[i, :, lanes]
 
-        return lax.fori_loop(0, ctx, collect, jnp.zeros((modes, LANES), F32)) * amplitude
+        return lax.fori_loop(0, ctx, collect, jnp.zeros((modes, LANES), F32))
 
     def extend_rows(g, carried, owner):
-        decay, step_factor = group_decay(g)
+        _, step_factor = group_decay(g)
         first = owner * rows
         factors = [spread(step_factor[m : m + 1]) for m in range(modes)]
-        ahead = place * steps + (first + 1).astype(F32)
-        fades = tuple(
-            spread(carried[m : m + 1]) * jnp.exp(-spread(decay[m : m + 1]) * ahead) for m in range(modes)
-        )
+        fades = tuple(spread(carried[m : m + 1]) * fading[owner, g, m] for m in range(modes))
 
         def extend(i, fades):
             rows_i = pl.ds(first + i, SUB, stride=steps)
@@ -411,6 +422,8 @@
             pltpu.VMEM((groups, tokens, LANES), F32),
             pltpu.VMEM((groups, modes, SUB, LANES), F32),
             pltpu.VMEM((n_ctx, modes, chans), F32),
+            pltpu.VMEM((modes, chans), F32),
+            pltpu.VMEM((2, groups, modes, SUB, LANES), F32),
             pltpu.VMEM((groups, tokens // 2, LANES), BF16),
             pltpu.VMEM((tokens // 2, 2 * chans), BF16),
             pltpu.VMEM((X_PIECES + Y_PIECES, 2, YS * rows, wide), BF16),

time: 31.6 us -> 30.9 us (0.978)
  the two profiles are of different devices: /device:TPU:2 before, /device:TPU:1 now
where the time goes in v6:
time: 30.9 us; the launch traced here: 30.3 us
  Pallas kernels  29.6 us (96%)
  local copies, waits for them, and re-layouts  0.71 us (2%)
    pallas_call x1, Pallas kernels, body(): pl.pallas_call(kernel, out_shape=pltpu.VMEM((rows, width), BF16), in_spec...  29.6 us
    unnamed x1, local copies, waits for them, and re-layouts  0.71 us

profile of v6, /device:TPU:1, one launch (start us, length us, event | category | flops | bytes accessed | tf_op | source)
XLA Modules:
  0.0 30.3 jit_solution(130411828409488167)
XLA Ops:
  0.0 29.6 %shard_map.73 = bf16[32,4096]{1,0:T(8,128)(2,1)S(1)} custom-call(bf16[512,256]{1,0:T(8,128)(2,1)} %in_hbm.1, bf16[512,256]{1,0:T(8,128)(2,1)} %val_hbm.1, bf16[512,256]{1,0:T(8,128)(2,1)} %gate_hbm.1, f32[16,256]{1,0:T(8,128)} %bitcast.3, f32[16,256]{1,0:T(8,128)} %bitcast.4, f32[1,256]{1,0:T(1,128)} %bitcast.5, bf16[256,4096]{1,0:T(8,128)(2,1)} %w_hbm.1), custom_call_target="tpu_custom_call" | custom-call | flops 1073741824 | bytes 4194304 | tf_op jit(solution)/shard_map/pallas_call | solution.py:408
  29.6 0.7 %copy.9 = bf16[32,4096]{1,0:T(8,128)(2,1)} copy(bf16[32,4096]{1,0:T(8,128)(2,1)S(1)} %shard_map.73) | data formatting | bytes 524288

commit v7 on v6

--- a/solution.py
+++ b/solution.py
@@ -142,7 +142,7 @@
         pltpu.make_async_remote_copy(
             src_ref=w_hbm.at[:, pl.ds(c * chunk, chunk)],
             dst_ref=w2.at[pl.ds(chans, chans), pl.ds(c * chunk, chunk)],
-            send_sem=pair_send.at[groups + c], recv_sem=pair_recv.at[groups + c],
+            send_sem=pair_send.at[1], recv_sem=pair_recv.at[groups + c],
             device_id=partner, device_id_type=MESH,
         )
         for c in range(W_CHUNKS)
@@ -221,7 +221,7 @@
             py[g, rows_i, :] = py[g, rows_i, :] + terms[0]
             return tuple(f * v for f, v in zip(factors, fades))
 
-        lax.fori_loop(0, rows, extend, fades, unroll=4)
+        lax.fori_loop(0, rows, extend, fades, unroll=8)
 
     g_copies = []
     carries = []
@@ -233,7 +233,7 @@
                 g_out[g, pl.ds((q * YS + r) * rows, rows), :] = gated_rows(target_block(r, q, 1 - core), g)
         g_copy = pltpu.make_async_remote_copy(
             src_ref=g_out.at[g], dst_ref=g2.at[:, pl.ds(chans + g * LANES, LANES)],
-            send_sem=pair_send.at[g], recv_sem=pair_recv.at[g],
+            send_sem=pair_send.at[0], recv_sem=pair_recv.at[g],
             device_id=partner, device_id_type=MESH,
         )
         g_copy.start()
@@ -282,7 +282,7 @@
         )
 
     def x_first(k):
-        turn = (k + 1) % 2
+        turn = int(k != 3)
         src = part.at[k, 0]
         return (
             1 + 2 * turn,
@@ -389,8 +389,11 @@
         def _(k=k):
             state_copy(k).wait_send()
 
-    for copy in w_copies + g_copies:
-        copy.wait_send()
+    for whole, sem in ((g_out, pair_send.at[0]), (w2.at[pl.ds(0, chans)], pair_send.at[1])):
+        pltpu.make_async_remote_copy(
+            src_ref=whole, dst_ref=whole, send_sem=sem, recv_sem=pair_recv.at[0],
+            device_id=partner, device_id_type=MESH,
+        ).wait_send()
     for kind, whole in enumerate((y_rel, y_dc, y_in, x_in, x_rel, x_dc)):
         send(whole, whole, kind, y_sem.at[0, 0], across).wait_send()
 
@@ -438,7 +441,7 @@
             dma((7,)),
             dma((n_ctx - 1,)),
             dma((n_ctx - 1,)),
-            dma((groups + W_CHUNKS,)),
+            dma((2,)),
             dma((groups + W_CHUNKS,)),
             dma((6,)),
             dma((3, X_PIECES)),

time: 30.9 us -> 30.7 us (level)
  no operation moved by 1% of the time
where the time goes in v7:
time: 30.7 us; the launch traced here: 30.3 us
  Pallas kernels  29.6 us (96%)
  local copies, waits for them, and re-layouts  0.71 us (2%)
    pallas_call x1, Pallas kernels, body(): pl.pallas_call(kernel, out_shape=pltpu.VMEM((rows, width), BF16), in_spec...  29.6 us
    unnamed x1, local copies, waits for them, and re-layouts  0.71 us

profile of v7, /device:TPU:1, one launch (start us, length us, event | category | flops | bytes accessed | tf_op | source)
XLA Modules:
  0.0 30.3 jit_solution(1996621533341973370)
XLA Ops:
  0.0 29.6 %shard_map.73 = bf16[32,4096]{1,0:T(8,128)(2,1)S(1)} custom-call(bf16[512,256]{1,0:T(8,128)(2,1)} %in_hbm.1, bf16[512,256]{1,0:T(8,128)(2,1)} %val_hbm.1, bf16[512,256]{1,0:T(8,128)(2,1)} %gate_hbm.1, f32[16,256]{1,0:T(8,128)} %bitcast.3, f32[16,256]{1,0:T(8,128)} %bitcast.4, f32[1,256]{1,0:T(1,128)} %bitcast.5, bf16[256,4096]{1,0:T(8,128)(2,1)} %w_hbm.1), custom_call_target="tpu_custom_call" | custom-call | flops 1073741824 | bytes 4194304 | tf_op jit(solution)/shard_map/pallas_call | solution.py:411
  29.6 0.7 %copy.9 = bf16[32,4096]{1,0:T(8,128)(2,1)} copy(bf16[32,4096]{1,0:T(8,128)(2,1)S(1)} %shard_map.73) | data formatting | bytes 524288

commit v8 on v7

--- a/solution.py
+++ b/solution.py
@@ -26,7 +26,7 @@
     x_in, x_rel, x_dc, y_rel, y_dc, y_out, y_in, acc,
     load_sem, st_send, st_recv, pair_send, pair_recv, sent, x_sem, y_sem,
 ):
-    tokens, chans = px.shape[1], px.shape[0] * LANES
+    tokens, chans = ig.shape
     steps = tokens // SUB
     modes = res_ref.shape[0]
     n_ctx = states.shape[0]
@@ -80,7 +80,7 @@
     for g in range(groups):
         lanes = pl.ds(g * LANES, LANES)
         product = (ig[:, lanes].astype(F32) * vs[:, lanes].astype(F32)).astype(BF16)
-        px[g] = product.astype(F32)
+        px[g, pl.ds(0, tokens), :] = product.astype(F32)
 
     def spread(row):
         return jnp.broadcast_to(row, (SUB, LANES))
@@ -421,8 +421,8 @@
             pltpu.VMEM((tokens, chans), BF16),
             pltpu.VMEM((tokens, chans), BF16),
             pltpu.VMEM((2 * chans, width), BF16),
-            pltpu.VMEM((groups, tokens, LANES), F32),
-            pltpu.VMEM((groups, tokens, LANES), F32),
+            pltpu.VMEM((groups, tokens + tokens // SUB, LANES), F32),
+            pltpu.VMEM((groups, tokens + tokens // SUB, LANES), F32),
             pltpu.VMEM((groups, modes, SUB, LANES), F32),
             pltpu.VMEM((n_ctx, modes, chans), F32),
             pltpu.VMEM((modes, chans), F32),

time: 30.7 us -> 30.7 us (level)
  no operation moved by 1% of the time
where the time goes in v8:
time: 30.7 us; the launch traced here: 30.3 us
  Pallas kernels  29.6 us (96%)
  local copies, waits for them, and re-layouts  0.71 us (2%)
    pallas_call x1, Pallas kernels, body(): pl.pallas_call(kernel, out_shape=pltpu.VMEM((rows, width), BF16), in_spec...  29.6 us
    unnamed x1, local copies, waits for them, and re-layouts  0.71 us

profile of v8, /device:TPU:1, one launch (start us, length us, event | category | flops | bytes accessed | tf_op | source)
XLA Modules:
  0.0 30.3 jit_solution(17976870249185293848)
XLA Ops:
  0.0 29.6 %shard_map.73 = bf16[32,4096]{1,0:T(8,128)(2,1)S(1)} custom-call(bf16[512,256]{1,0:T(8,128)(2,1)} %in_hbm.1, bf16[512,256]{1,0:T(8,128)(2,1)} %val_hbm.1, bf16[512,256]{1,0:T(8,128)(2,1)} %gate_hbm.1, f32[16,256]{1,0:T(8,128)} %bitcast.3, f32[16,256]{1,0:T(8,128)} %bitcast.4, f32[1,256]{1,0:T(1,128)} %bitcast.5, bf16[256,4096]{1,0:T(8,128)(2,1)} %w_hbm.1), custom_call_target="tpu_custom_call" | custom-call | flops 1073741824 | bytes 4194304 | tf_op jit(solution)/shard_map/pallas_call | solution.py:411
  29.6 0.7 %copy.9 = bf16[32,4096]{1,0:T(8,128)(2,1)} copy(bf16[32,4096]{1,0:T(8,128)(2,1)S(1)} %shard_map.73) | data formatting | bytes 524288
